TPU v7x, 256 devices: a whole 4x4x8 slice. The times are simulated.
256 devices in a mesh: aux: 64 (over z, y, x_lo), rows: 4 (over x_hi, core).
Axes of the slice: x: 4 (x_hi: 2, x_lo: 2; x = x_hi * 2 + x_lo), y: 4, z: 8, core: 2. Of those that a mesh axis runs over, the one named last changes fastest.
Arguments:
- half_ints: bfloat16 [192, 500, 4096], P('aux', None, 'rows'), may hold values from -0.109375 to 0.109375
Outputs:
- exchange_matrix: float32 [1024, 4, 4096], P('aux', None, 'rows')
All inputs are finite; a program needn't handle non-finite values.
Results may differ from a plain program's by a relative error of at most 0.0023.
Values may be sent and summed in bfloat16 or wider, within the bound.
A program may use at most 192 MiB of HBM per device.

v0:
```python
import jax
import jax.numpy as jnp
from jax import lax
from jax.sharding import PartitionSpec as P


def reduce_full(partial_term, slab_rows, row_count, block_width):
    summed = lax.psum_scatter(
        partial_term(jnp.int32(0), slab_rows * lax.axis_size("aux")),
        "aux",
        scatter_dimension=0,
        tiled=True,
    )
    return summed.reshape(slab_rows, row_count, block_width)


def shards(half_ints):
    gathered = lax.all_gather(half_ints, "rows", axis=2, tiled=True)
    block_width = half_ints.shape[2]
    row_count = lax.axis_size("rows")
    slab_rows = block_width // lax.axis_size("aux")
    blocks = gathered.reshape(gathered.shape[0], gathered.shape[1], row_count, block_width)

    def partial_term(start, count):
        product = jnp.einsum("pisc,pin->csn", blocks, half_ints, preferred_element_type=jnp.float32)
        return product.reshape(count, row_count * block_width)

    gram_part = reduce_full(partial_term, slab_rows, row_count, block_width)
    return -0.5 * gram_part


def solution(mesh):
    placed = (P("aux", None, "rows"),)
    return jax.shard_map(
        shards, mesh=mesh, in_specs=placed, out_specs=P("aux", None, "rows"), check_vma=False
    )
```

profile of v0, /device:TPU:1, one launch (start us, length us, event | category | flops | bytes accessed | tf_op | source)
XLA Modules:
  0.0 535.7 jit_solution(7928370804345257661)
XLA Ops:
  6.5 0.0 all-gather.2.cloned.1.call-start
  6.5 0.7 all-gather.2.cloned.1.call-update
  7.3 0.0 copy-start
  7.3 0.0 reduce-scatter.4.cloned.1.call-start
  7.3 93.7 %all-gather.2.cloned.1.call-done = bf16[3,500,4096]{2,1,0:T(8,128)(2,1)} async-done(((bf16[3,500,1024]{2,1,0:T(8,128)(2,1)}), bf16[3,500,4096]{2,1,0:T(8,128)(2,1)}) %all-gather.2.cloned.1.call-update) | async-done | bytes 12288016 | tf_op jit(solution)/shard_map/all_gather | solution.py:18
  101.0 16.6 %copy.6 = bf16[3,500,4096]{1,2,0:T(8,128)(2,1)} copy(bf16[3,500,4096]{2,1,0:T(8,128)(2,1)} %all-gather.2.cloned.1.call-done) | data formatting | bytes 24576000 | tf_op jit(solution)/shard_map/all_gather | solution.py:18
  117.6 0.0 copy-done
  117.6 19.5 %fusion = f32[1024,4,1024,1]{2,0,1,3:T(8,128)} fusion(bf16[3,500,4,1024]{1,3,2,0:T(8,128)(2,1)} %bitcast.18, bf16[3,500,1024]{2,1,0:T(8,128)(2,1)S(1)} %copy-done), kind=kOutput, calls=%fused_computation | convolution fusion | flops 12582912000 | bytes 32137216 | tf_op jit(solution)/shard_map/pisc,pin->csn/dot_general | solution.py:25
  137.1 17.4 %copy.12 = f32[1024,4096]{1,0:T(8,128)} copy(f32[1024,4096]{0,1:T(8,128)} %bitcast.17) | data formatting | bytes 33554432
  154.6 0.0 reduce-scatter.4.cloned.1.call-update
  154.6 368.3 %reduce-scatter.4.cloned.1.call-done = f32[16,4096]{1,0:T(8,128)} async-done(((f32[1024,4096]{1,0:T(8,128)}), f32[16,4096]{1,0:T(8,128)}) %reduce-scatter.4.cloned.1.call-update) | async-done | bytes 262160
  522.9 1.5 copy.13
  524.4 1.5 broadcast_multiply_fusion
  525.9 2.9 copy.8
Async XLA Ops:
  6.5 94.5 %all-gather.2.cloned.1.call-start = ((), (), s32[]{:S(2)}) async-start(), calls=%async_computation.1 | async-start | bytes 15482880 | tf_op jit(solution)/shard_map/all_gather | solution.py:18
  7.3 110.4 %copy-start = (bf16[3,500,1024]{2,1,0:T(8,128)(2,1)S(1)}, bf16[3,500,1024]{2,1,0:T(8,128)(2,1)}, u32[]{:S(2)}) copy-start(bf16[3,500,1024]{2,1,0:T(8,128)(2,1)} %param.1) | copy-start | bytes 9216004
  7.3 515.6 %reduce-scatter.4.cloned.1.call-start = ((), (), s32[]{:S(2)}) async-start(), calls=%async_computation.2 | async-start | bytes 17039360
Sparse Core Ops, SparseCore 0:
  9.2 91.7 all-gather.1
  154.7 368.1 reduce-scatter.3
where the time goes:
time: 537 us; the launch traced here: 536 us
  waiting for transfers between devices  463 us (86%)
  local copies, waits for them, and re-layouts  38.5 us (7%)
  matrix products  19.5 us (4%)
  between operations  13.4 us (2%)
    unnamed x3, waiting for transfers between devices  369 us
    all_gather x1, waiting for transfers between devices, shards(): gathered = lax.all_gather(half_ints, 'rows', axis=2, tiled=True)  93.7 us
    dot_general x1, matrix products, partial_term(): jnp.einsum('pisc,pin->csn', blocks, half_ints, preferred_element_type=jnp...  19.5 us
    unnamed x4, local copies, waits for them, and re-layouts  19 us
    all_gather x1, local copies, waits for them, and re-layouts, shards(): gathered = lax.all_gather(half_ints, 'rows', axis=2, tiled=True)  16.6 us
  transfers between devices with their start and end apart: 2, of which 2 were waited for; matrix products, arithmetic and copies ran while one was open for 0% of the time, Pallas kernels for 0%

commit v1 on v0

v1 whole, which is shorter than its diff:
```python
import functools

import jax
import jax.numpy as jnp
from jax import lax
from jax.experimental import pallas as pl
from jax.experimental.pallas import tpu as pltpu
from jax.sharding import PartitionSpec as P

MESH = pl.DeviceIdType.MESH
BF = jnp.bfloat16
F32 = jnp.float32
NZ, NY = 8, 4
W = 1024
K = 1536
KH = K // 2


class Ring:
    def __init__(self, size, pos, device_at, buf, recv, send_sem, recv_sem):
        self.size, self.pos, self.buf, self.recv = size, pos, buf, recv
        self.peers = (device_at(lax.rem(pos + 1, size)), device_at(lax.rem(pos + size - 1, size)))
        self.send_sem, self.recv_sem = send_sem, recv_sem
        self.m, self.rows, self.lanes = buf.shape[2:]

    def where(self, direction, i):
        distance = self.size // 2 - (i + 1) // 2
        half = (i + direction) % 2
        chunk = lax.rem(self.pos + (distance if direction == 0 else self.size - distance), self.size)
        return chunk, half

    def copy(self, direction, i):
        chunk, half = self.where(direction, i)
        return pltpu.make_async_remote_copy(
            src_ref=self.buf.at[chunk, half],
            dst_ref=self.recv.at[direction, i],
            send_sem=self.send_sem.at[direction, i],
            recv_sem=self.recv_sem.at[direction, i],
            device_id=self.peers[direction],
            device_id_type=MESH,
        )

    def step(self, i):
        for direction in range(2):
            if i >= 2:
                self.copy(direction, i - 2).wait_recv()
                chunk, half = self.where(direction, i)
                self.add(chunk, half, direction, i - 2)
            self.copy(direction, i).start()

    def add(self, chunk, half, direction, i):
        rows = min(self.rows, 32 if self.lanes == W else 128)
        parts = self.rows // rows

        def body(t, _):
            a, b = t // parts, pl.multiple_of((t % parts) * rows, rows)
            at = (chunk, half, a, pl.ds(b, rows))
            total = self.buf[at].astype(F32) + self.recv[direction, i, a, pl.ds(b, rows)].astype(F32)
            self.buf[at] = total.astype(self.buf.dtype)
            return _

        lax.fori_loop(0, self.m * parts, body, 0)

    def finish(self, put):
        last = self.size - 2
        for direction in range(2):
            self.copy(direction, last - 1).wait_recv()
            self.copy(direction, last).wait_recv()
        for half in range(2):
            up, down = (last, last - 1) if half == 0 else (last - 1, last)

            def body(t, _, half=half, up=up, down=down):
                a, side = t // 2, t % 2
                rows = self.rows // 2
                r = pl.ds(pl.multiple_of(side * rows, rows), rows)
                total = (
                    self.buf[self.pos, half, a, r].astype(F32)
                    + self.recv[0, up, a, r].astype(F32)
                    + self.recv[1, down, a, r].astype(F32)
                )
                put(half * self.m + a, side, total)
                return _

            lax.fori_loop(0, self.m * 2, body, 0)

    def drain(self):
        for direction in range(2):
            for i in range(self.size - 1):
                self.copy(direction, i).wait_send()


def gram_tiles(lhs, rhs, put):
    def body(t, _):
        i, j = t // 2, t % 2
        left = lhs[:, pl.ds(pl.multiple_of(i * 256, 256), 256)]
        right = rhs[:, pl.ds(pl.multiple_of(j * 512, 512), 512)]
        tile = lax.dot_general(left, right, (((0,), (0,)), ((), ())), preferred_element_type=F32)
        put(i, j, tile.astype(BF))
        return _

    lax.fori_loop(0, 8, body, 0)


def kernel(
    x_ref, out_ref, mate_x, got, mate_got,
    dy, dz, qz, qy, e1, e2, h1, h2,
    dy_r, dz_r, qz_r, qy_r, e1_r, e2_r, h1_r, h2_r,
    ef1, ef2, ef_r, t1, t2, mix, mix_r, summed, pieces,
    dy_s, dy_t, dz_s, dz_t, qz_s, qz_t, qy_s, qy_t, e1_s, e1_t, e2_s, e2_t, h1_s, h1_t, h2_s, h2_t,
    x_s, x_t, mate_s, mate_t, ef_s, ef_t, mix_s, mix_t, piece_s, piece_t,
):
    a = lax.axis_index("aux")
    r = lax.axis_index("rows")
    z, y, l = a // 8, (a // 2) % 4, a % 2
    h, c = r // 2, r % 2
    x = 2 * h + l

    def dev(x_, y_, z_, c_):
        return (z_ * 8 + y_ * 2 + x_ % 2, 2 * (x_ // 2) + c_)

    def on_x(step):
        return dev(lax.rem(x + step, 4), y, z, c)

    mate = dev(x, y, z, 1 - c)

    barrier = pltpu.get_barrier_semaphore()
    partners = [mate] + [on_x(d) for d in (1, 2, 3)]
    partners += [dev(x, y, lax.rem(z + d, NZ), c) for d in range(1, NZ)]
    partners += [dev(x, lax.rem(y + d, NY), z, c_) for d in range(1, NY) for c_ in range(2)]
    for partner in partners:
        pl.semaphore_signal(barrier, inc=1, device_id=partner, device_id_type=MESH)
    pl.semaphore_wait(barrier, len(partners))

    def remote(src, dst, send, recv, device):
        return pltpu.make_async_remote_copy(
            src_ref=src, dst_ref=dst, send_sem=send, recv_sem=recv, device_id=device, device_id_type=MESH
        )

    def x_copy(k, step):
        target_h = lax.rem(x + step, 4) // 2
        rows = pl.ds(pl.multiple_of(target_h * KH, KH), KH)
        return remote(x_ref.at[rows], got.at[h], x_s.at[k], x_t.at[h], on_x(step))

    x_copies = [x_copy(0, 1), x_copy(1, 3)]
    for copy in x_copies:
        copy.start()
    mate_copy = remote(x_ref, mate_x, mate_s.at[0], mate_t.at[0], mate)
    mate_copy.start()

    def z_ring(*refs):
        return Ring(NZ, z, lambda p: dev(x, y, p, c), *refs)

    def y_ring(*refs):
        return Ring(NY, y, lambda p: dev(x, p, z, c), *refs)

    ring_dy = y_ring(dy, dy_r, dy_s, dy_t)
    ring_dz = z_ring(dz, dz_r, dz_s, dz_t)
    ring_e1 = z_ring(e1, e1_r, e1_s, e1_t)
    ring_e2 = y_ring(e2, e2_r, e2_s, e2_t)
    ring_qz = z_ring(qz, qz_r, qz_s, qz_t)
    ring_qy = y_ring(qy, qy_r, qy_s, qy_t)
    ring_h1 = y_ring(h1, h1_r, h1_s, h1_t)
    ring_h2 = z_ring(h2, h2_r, h2_s, h2_t)

    def put_dy(i, j, tile):
        for k in range(2):
            zi = 2 * i + k
            for yi in range(4):
                rows = tile[k * 128 + yi * 32 : k * 128 + yi * 32 + 32]
                dy[yi, zi // 4, zi % 4, :, pl.ds(pl.multiple_of(j * 512, 512), 512)] = rows

    def put_dz(i, j, tile):
        for k in range(2):
            for yi in range(4):
                rows = tile[k * 128 + yi * 32 : k * 128 + yi * 32 + 32]
                dz[2 * i + k, yi // 2, yi % 2, :, pl.ds(pl.multiple_of(j * 512, 512), 512)] = rows

    def put_qz(i, j, tile):
        for k in range(2):
            for yi in range(4):
                for n in range(4):
                    rows = tile[k * 128 + yi * 32 : k * 128 + yi * 32 + 32, n * 128 : n * 128 + 128]
                    qz[j * 4 + n, yi // 2, yi % 2, pl.ds(pl.multiple_of((2 * i + k) * 32, 32), 32), :] = rows

    def put_qy(i, j, tile):
        for k in range(2):
            for yi in range(4):
                for n in range(4):
                    rows = tile[k * 128 + yi * 32 : k * 128 + yi * 32 + 32, n * 128 : n * 128 + 128]
                    qy[yi, j, n, pl.ds(pl.multiple_of((2 * i + k) * 32, 32), 32), :] = rows

    def put_e1(n, side, total):
        e1[n, side, 0] = total

    def put_e2(n, side, total):
        e2[n, side, 0] = total

    def put_h1(n, side, total):
        h1[n, side, 0] = total

    def put_h2(n, side, total):
        h2[n, side, 0] = total

    gram_tiles(x_ref, x_ref, put_dy)
    ring_dy.step(0)
    ring_dy.step(1)
    mate_copy.wait_recv()
    gram_tiles(mate_x, x_ref, put_dz)
    ring_dz.step(0)
    ring_dz.step(1)
    ring_dy.step(2)
    for i in (2, 3, 4):
        ring_dz.step(i)
    ring_dy.finish(put_e1)
    ring_e1.step(0)
    ring_e1.step(1)
    ring_dz.step(5)
    ring_dz.step(6)
    ring_e1.step(2)
    ring_e1.step(3)
    ring_dz.finish(put_e2)
    ring_e2.step(0)
    ring_e2.step(1)

    for slot in range(2):
        remote(x_ref.at[pl.ds(0, KH)], got.at[slot], x_s.at[0], x_t.at[slot], mate).wait_recv()
    mate_got_copy = remote(got.at[0], mate_got, mate_s.at[1], mate_t.at[1], mate)
    mate_got_copy.start()
    gram_tiles(got.at[0], got.at[1], put_qz)
    ring_qz.step(0)
    ring_qz.step(1)
    mate_got_copy.wait_recv()
    gram_tiles(mate_got, got.at[1], put_qy)
    ring_qy.step(0)
    ring_qy.step(1)

    ring_e1.step(4)
    ring_e2.step(2)
    ring_e1.step(5)
    ring_e1.step(6)

    def put_ef(ref):
        def put(half, part, total):
            rows = ref.shape[1] // 2
            ref[half, pl.ds(pl.multiple_of(part * rows, rows), rows), :] = total

        return put

    ring_qz.step(2)
    ring_qz.step(3)
    ring_qy.step(2)
    ring_e1.finish(put_ef(ef1))
    ring_e2.finish(put_ef(ef2))

    near = dev(2 * h + (1 - l), y, z, c)
    ef_copies = [
        remote(ref.at[1 - l], ef_r.at[k], ef_s.at[k], ef_t.at[k], near) for k, ref in enumerate((ef1, ef2))
    ]
    for copy in ef_copies:
        copy.start()

    ring_qz.step(4)
    ring_qz.step(5)
    ring_qy.finish(put_h2)
    ring_h2.step(0)
    ring_h2.step(1)
    ring_qz.step(6)
    ring_h2.step(2)
    ring_h2.step(3)
    ring_qz.finish(put_h1)
    ring_h1.step(0)
    ring_h1.step(1)
    ring_h2.step(4)
    ring_h2.step(5)
    ring_h1.step(2)
    ring_h2.step(6)
    for k, ref in enumerate((ef1, ef2)):
        ef_copies[k].wait_recv()
        block = 2 * h + (c if k == 0 else 1 - c)
        out_ref[block] = -0.5 * (ref[l] + ef_r[k])
    ring_h1.finish(put_ef(t1))
    ring_h2.finish(put_ef(t2))

    for tile, b in ((t1, c), (t2, 1 - c)):
        for half in range(2):
            block = tile[half]
            flipped = block.T
            for n in range(4):
                for side in range(2):
                    at = n * 32 + side * 16
                    mix[2 + side, half * 4 + n, b] = block[at : at + 16]
                    mix[side, n * 2 + b, half] = flipped[at : at + 16]
    mix_copies = [
        remote(mix.at[lax.rem(x + d, 4)], mix_r.at[d - 1], mix_s.at[d - 1], mix_t.at[d - 1], on_x(d)) for d in (1, 2, 3)
    ]
    for copy in mix_copies:
        copy.start()
    for copy in mix_copies:
        copy.wait_recv()
    mine = z * h + (y * 2 + c) * (1 - h)
    for n in range(8):
        summed[n] = -0.5 * ((mix[x, n] + mix_r[0, n]) + (mix_r[1, n] + mix_r[2, n]))
    pieces[mine] = summed[mine]

    def piece_copy(d):
        n = lax.rem(mine + d, 8)
        target = dev(x, y * h + (n // 2) * (1 - h), n * h + z * (1 - h), c * h + (n % 2) * (1 - h))
        return remote(summed.at[n], pieces.at[mine], piece_s.at[d - 1], piece_t.at[d - 1], target)

    piece_copies = [piece_copy(d) for d in range(1, 8)]
    for copy in piece_copies:
        copy.start()
    for copy in piece_copies:
        copy.wait_recv()

    @pl.when(h == 1)
    def _():
        for s in range(2):
            for n in range(8):
                out_ref[s, :, n * 128 : n * 128 + 128] = pieces[n, s]

    @pl.when(h == 0)
    def _():
        for s in range(2):
            for n in range(8):
                at = (n % 4) * 32
                parts = [pieces[v * 2 + s, n // 4][:, at : at + 32] for v in range(4)]
                out_ref[2 + s, :, n * 128 : n * 128 + 128] = jnp.concatenate(parts, axis=1)

    for ring in (ring_dy, ring_dz, ring_e1, ring_e2, ring_qz, ring_qy, ring_h1, ring_h2):
        ring.drain()
    for copy in x_copies + [mate_copy, mate_got_copy] + ef_copies + mix_copies + piece_copies:
        copy.wait_send()


def shards(half_ints):
    x = jnp.pad(half_ints, ((0, 0), (0, K // 3 - half_ints.shape[1]), (0, 0))).reshape(K, W)
    dma = pltpu.SemaphoreType.DMA
    bufs = [
        ((NY, 2, 4, 32, W), BF), ((NZ, 2, 2, 32, W), BF), ((NZ, 2, 2, 256, 128), BF), ((NY, 2, 4, 256, 128), BF),
        ((NZ, 2, 1, 16, W), F32), ((NY, 2, 1, 16, W), F32), ((NY, 2, 1, 128, 128), F32), ((NZ, 2, 1, 128, 128), F32),
    ]
    recvs = [((2, shape[0] - 1) + shape[2:], dtype) for shape, dtype in bufs]
    scratch = [pltpu.VMEM((K, W), BF), pltpu.VMEM((2, KH, W), BF), pltpu.VMEM((KH, W), BF)]
    scratch += [pltpu.VMEM(shape, dtype) for shape, dtype in bufs + recvs]
    scratch += [pltpu.VMEM((2, 16, W), F32)] * 3
    scratch += [pltpu.VMEM((2, 128, 128), F32)] * 2
    scratch += [
        pltpu.VMEM((4, 8, 2, 16, 128), F32),
        pltpu.VMEM((3, 8, 2, 16, 128), F32),
        pltpu.VMEM((8, 2, 16, 128), F32),
        pltpu.VMEM((8, 2, 16, 128), F32),
    ]
    for shape, _ in bufs:
        scratch += [dma((2, shape[0] - 1))] * 2
    scratch += [dma((2,))] * 6 + [dma((3,))] * 2 + [dma((7,))] * 2
    out = pl.pallas_call(
        kernel,
        out_shape=jax.ShapeDtypeStruct((4, 16, W), F32),
        in_specs=[pl.BlockSpec(memory_space=pltpu.VMEM)],
        out_specs=pl.BlockSpec(memory_space=pltpu.VMEM),
        scratch_shapes=scratch,
        compiler_params=pltpu.CompilerParams(
            collective_id=0, has_side_effects=True, vmem_limit_bytes=56 * 1024 * 1024
        ),
        cost_estimate=pl.CostEstimate(flops=2 * 1024 * 1024 * K * 3, bytes_accessed=4 << 20, transcendentals=0),
    )(x)
    return out.transpose(1, 0, 2)


def solution(mesh):
    placed = (P("aux", None, "rows"),)
    return jax.shard_map(
        shards, mesh=mesh, in_specs=placed, out_specs=P("aux", None, "rows"), check_vma=False
    )
```

time: 537 us -> 112 us (0.21)
  waiting for transfers between devices: 463 us -> 0 us
  Pallas kernels: 0 us -> 106 us
  local copies, waits for them, and re-layouts: 38.5 us -> 5.8 us
  matrix products: 19.5 us -> 0 us
  between operations: 13.4 us -> 0.01 us
    unnamed x3 -> x0, waiting for transfers between devices: 369 us -> none
    pallas_call x0 -> x1, Pallas kernels: none -> 106 us  [shards(): pl.pallas_call(kernel, out_shape=jax.ShapeDtypeStruct((4, 16, W), F32), i...]
    all_gather x1 -> x0, waiting for transfers between devices: 93.7 us -> none  [shards(): gathered = lax.all_gather(half_ints, 'rows', axis=2, tiled=True)]
    dot_general x1 -> x0, matrix products: 19.5 us -> none  [partial_term(): jnp.einsum('pisc,pin->csn', blocks, half_ints, preferred_element_type=jnp...]
    unnamed x4 -> x0, local copies, waits for them, and re-layouts: 19 us -> none
    all_gather x1 -> x0, local copies, waits for them, and re-layouts: 16.6 us -> none  [shards(): gathered = lax.all_gather(half_ints, 'rows', axis=2, tiled=True)]
  transfers between devices with their start and end apart: 2 -> 0, of which waited for: 2 -> 0; matrix products, arithmetic and copies ran while one was open for 0% -> 0% of each run, Pallas kernels for 0% -> 0%
where the time goes in v1:
time: 112 us
  Pallas kernels  106 us (95%)
  local copies, waits for them, and re-layouts  5.8 us (5%)
    pallas_call x1, Pallas kernels, shards(): pl.pallas_call(kernel, out_shape=jax.ShapeDtypeStruct((4, 16, W), F32), i...  106 us
    pad x1, local copies, waits for them, and re-layouts, shards(): jnp.pad(half_ints, ((0, 0), (0, K // 3 - half_ints.shape[1]), (0, 0)))  3.97 us

profile of v1, /device:TPU:1, one launch (start us, length us, event | category | flops | bytes accessed | tf_op | source)
XLA Modules:
  0.0 112.2 jit_solution(15445074402666363189)
XLA Ops:
  0.0 4.0 %pad.4 = bf16[3,512,1024]{2,1,0:T(8,128)(2,1)} pad(bf16[3,500,1024]{2,1,0:T(8,128)(2,1)} %param.1, bf16[]{:T(256)} %constant.2.clone.1), padding=0_0x0_12x0_0 | pad | bytes 6217730 | tf_op jit(solution)/shard_map/jit(_pad)/pad | solution.py:337
  4.0 106.4 %shard_map.17 = f32[4,16,1024]{2,1,0:T(8,128)} custom-call(bf16[1536,1024]{1,0:T(8,128)(2,1)} %bitcast.2), custom_call_target="tpu_custom_call" | custom-call | flops 9663676416 | bytes 4194304 | tf_op jit(solution)/shard_map/pallas_call | solution.py:357
  110.4 1.8 %copy.2 = f32[16,4,1024]{2,1,0:T(4,128)} copy(f32[16,4,1024]{2,0,1:T(8,128)} %bitcast.3) | data formatting | bytes 524288 | tf_op jit(solution)/shard_map/transpose | solution.py:368

commit v2 on v1

--- a/solution.py
+++ b/solution.py
@@ -14,6 +14,7 @@
 W = 1024
 K = 1536
 KH = K // 2
+OCC = 500
 
 
 class Ring:
@@ -61,7 +62,7 @@
 
         lax.fori_loop(0, self.m * parts, body, 0)
 
-    def finish(self, put):
+    def finish(self, put, sides=1):
         last = self.size - 2
         for direction in range(2):
             self.copy(direction, last - 1).wait_recv()
@@ -70,8 +71,8 @@
             up, down = (last, last - 1) if half == 0 else (last - 1, last)
 
             def body(t, _, half=half, up=up, down=down):
-                a, side = t // 2, t % 2
-                rows = self.rows // 2
+                a, side = t // sides, t % sides
+                rows = self.rows // sides
                 r = pl.ds(pl.multiple_of(side * rows, rows), rows)
                 total = (
                     self.buf[self.pos, half, a, r].astype(F32)
@@ -81,7 +82,7 @@
                 put(half * self.m + a, side, total)
                 return _
 
-            lax.fori_loop(0, self.m * 2, body, 0)
+            lax.fori_loop(0, self.m * sides, body, 0)
 
     def drain(self):
         for direction in range(2):
@@ -95,20 +96,23 @@
         left = lhs[:, pl.ds(pl.multiple_of(i * 256, 256), 256)]
         right = rhs[:, pl.ds(pl.multiple_of(j * 512, 512), 512)]
         tile = lax.dot_general(left, right, (((0,), (0,)), ((), ())), preferred_element_type=F32)
-        put(i, j, tile.astype(BF))
+        put(i, j, tile)
         return _
 
     lax.fori_loop(0, 8, body, 0)
 
 
 def kernel(
-    x_ref, out_ref, mate_x, got, mate_got,
+    half_ints, out_ref, raw, x_ref, mate_x, got, mate_got,
     dy, dz, qz, qy, e1, e2, h1, h2,
     dy_r, dz_r, qz_r, qy_r, e1_r, e2_r, h1_r, h2_r,
-    ef1, ef2, ef_r, t1, t2, mix, mix_r, summed, pieces,
+    ef1, ef2, ef_r, t1, t2, mix, mix_b, mix_r, summed, pieces, diag, diag_sum, diag_y, diag_z,
     dy_s, dy_t, dz_s, dz_t, qz_s, qz_t, qy_s, qy_t, e1_s, e1_t, e2_s, e2_t, h1_s, h1_t, h2_s, h2_t,
-    x_s, x_t, mate_s, mate_t, ef_s, ef_t, mix_s, mix_t, piece_s, piece_t,
+    raw_t, x_s, x_t, mate_s, mate_t, ef_s, ef_t, mix_s, mix_t, piece_s, piece_t, dgy_s, dgy_t, dgz_s, dgz_t,
 ):
+    raw_copies = [pltpu.make_async_copy(half_ints.at[p], raw.at[p], raw_t.at[p]) for p in range(3)]
+    for copy in raw_copies:
+        copy.start()
     a = lax.axis_index("aux")
     r = lax.axis_index("rows")
     z, y, l = a // 8, (a // 2) % 4, a % 2
@@ -124,11 +128,23 @@
     mate = dev(x, y, z, 1 - c)
 
     barrier = pltpu.get_barrier_semaphore()
-    partners = [mate] + [on_x(d) for d in (1, 2, 3)]
-    partners += [dev(x, y, lax.rem(z + d, NZ), c) for d in range(1, NZ)]
-    partners += [dev(x, lax.rem(y + d, NY), z, c_) for d in range(1, NY) for c_ in range(2)]
+    partners = [mate, on_x(1), on_x(3)]
+    partners += [dev(x, y, lax.rem(z + d, NZ), c) for d in (1, NZ - 1)]
+    partners += [dev(x, lax.rem(y + d, NY), z, c) for d in (1, NY - 1)]
     for partner in partners:
         pl.semaphore_signal(barrier, inc=1, device_id=partner, device_id_type=MESH)
+    whole = OCC // 16 * 16
+    for p in range(3):
+        raw_copies[p].wait()
+
+        def body(t, _, p=p):
+            rows = pl.multiple_of(t * 16, 16)
+            x_ref[pl.ds(p * 512 + rows, 16), :] = raw[p, pl.ds(rows, 16), :]
+            return _
+
+        lax.fori_loop(0, whole // 16, body, 0)
+        tail = jnp.zeros((512 - OCC, W), BF)
+        x_ref[p * 512 + whole : p * 512 + 512, :] = jnp.concatenate([raw[p, whole:OCC, :], tail], axis=0)
     pl.semaphore_wait(barrier, len(partners))
 
     def remote(src, dst, send, recv, device):
@@ -163,6 +179,11 @@
     ring_h2 = z_ring(h2, h2_r, h2_s, h2_t)
 
     def put_dy(i, j, tile):
+        on_diagonal = lax.broadcasted_iota(jnp.int32, (256, 512), 1) - lax.broadcasted_iota(jnp.int32, (256, 512), 0)
+        on_diagonal = on_diagonal == i * 256 - j * 512
+        columns = pl.ds(pl.multiple_of(j * 512, 512), 512)
+        diag[:, columns] += jnp.sum(jnp.where(on_diagonal, tile, 0.0), axis=0, keepdims=True)
+        tile = jnp.where(on_diagonal, 0.0, tile).astype(BF)
         for k in range(2):
             zi = 2 * i + k
             for yi in range(4):
@@ -170,12 +191,14 @@
                 dy[yi, zi // 4, zi % 4, :, pl.ds(pl.multiple_of(j * 512, 512), 512)] = rows
 
     def put_dz(i, j, tile):
+        tile = tile.astype(BF)
         for k in range(2):
             for yi in range(4):
                 rows = tile[k * 128 + yi * 32 : k * 128 + yi * 32 + 32]
                 dz[2 * i + k, yi // 2, yi % 2, :, pl.ds(pl.multiple_of(j * 512, 512), 512)] = rows
 
     def put_qz(i, j, tile):
+        tile = tile.astype(BF)
         for k in range(2):
             for yi in range(4):
                 for n in range(4):
@@ -183,6 +206,7 @@
                     qz[j * 4 + n, yi // 2, yi % 2, pl.ds(pl.multiple_of((2 * i + k) * 32, 32), 32), :] = rows
 
     def put_qy(i, j, tile):
+        tile = tile.astype(BF)
         for k in range(2):
             for yi in range(4):
                 for n in range(4):
@@ -190,17 +214,18 @@
                     qy[yi, j, n, pl.ds(pl.multiple_of((2 * i + k) * 32, 32), 32), :] = rows
 
     def put_e1(n, side, total):
-        e1[n, side, 0] = total
+        e1[n, side, 0] = total.astype(BF)
 
     def put_e2(n, side, total):
-        e2[n, side, 0] = total
+        e2[n, side, 0] = total.astype(BF)
 
     def put_h1(n, side, total):
-        h1[n, side, 0] = total
+        h1[n, side, 0] = total.astype(BF)
 
     def put_h2(n, side, total):
-        h2[n, side, 0] = total
-
+        h2[n, side, 0] = total.astype(BF)
+
+    diag[...] = jnp.zeros_like(diag)
     gram_tiles(x_ref, x_ref, put_dy)
     ring_dy.step(0)
     ring_dy.step(1)
@@ -211,14 +236,29 @@
     ring_dy.step(2)
     for i in (2, 3, 4):
         ring_dz.step(i)
-    ring_dy.finish(put_e1)
+    ring_dy.finish(put_e1, 2)
+    dgy_copies = [
+        remote(diag, diag_y.at[d - 1], dgy_s.at[d - 1], dgy_t.at[d - 1], dev(x, lax.rem(y + d, NY), z, c))
+        for d in range(1, NY)
+    ]
+    for copy in dgy_copies:
+        copy.start()
     ring_e1.step(0)
     ring_e1.step(1)
     ring_dz.step(5)
     ring_dz.step(6)
     ring_e1.step(2)
     ring_e1.step(3)
-    ring_dz.finish(put_e2)
+    ring_dz.finish(put_e2, 2)
+    for copy in dgy_copies:
+        copy.wait_recv()
+    diag_sum[...] = (diag[...] + diag_y[0]) + (diag_y[1] + diag_y[2])
+    dgz_copies = [
+        remote(diag_sum, diag_z.at[d - 1], dgz_s.at[d - 1], dgz_t.at[d - 1], dev(x, y, lax.rem(z + d, NZ), c))
+        for d in range(1, NZ)
+    ]
+    for copy in dgz_copies:
+        copy.start()
     ring_e2.step(0)
     ring_e2.step(1)
 
@@ -241,8 +281,7 @@
 
     def put_ef(ref):
         def put(half, part, total):
-            rows = ref.shape[1] // 2
-            ref[half, pl.ds(pl.multiple_of(part * rows, rows), rows), :] = total
+            ref[half] = total
 
         return put
 
@@ -250,6 +289,15 @@
     ring_qz.step(3)
     ring_qy.step(2)
     ring_e1.finish(put_ef(ef1))
+    for copy in dgz_copies:
+        copy.wait_recv()
+    total_diag = diag_sum[...]
+    for d in range(NZ - 1):
+        total_diag = total_diag + diag_z[d]
+    for side in range(2):
+        row = lax.broadcasted_iota(jnp.int32, (16, W), 0) + (z * 128 + y * 32 + side * 16)
+        own = lax.broadcasted_iota(jnp.int32, (16, W), 1) == row
+        ef1[side] += jnp.where(own, total_diag, 0.0)
     ring_e2.finish(put_ef(ef2))
 
     near = dev(2 * h + (1 - l), y, z, c)
@@ -261,45 +309,58 @@
 
     ring_qz.step(4)
     ring_qz.step(5)
-    ring_qy.finish(put_h2)
+    ring_qy.finish(put_h2, 2)
     ring_h2.step(0)
     ring_h2.step(1)
     ring_qz.step(6)
     ring_h2.step(2)
     ring_h2.step(3)
-    ring_qz.finish(put_h1)
+    ring_qz.finish(put_h1, 2)
     ring_h1.step(0)
     ring_h1.step(1)
     ring_h2.step(4)
     ring_h2.step(5)
     ring_h1.step(2)
-    ring_h2.step(6)
     for k, ref in enumerate((ef1, ef2)):
         ef_copies[k].wait_recv()
         block = 2 * h + (c if k == 0 else 1 - c)
         out_ref[block] = -0.5 * (ref[l] + ef_r[k])
-    ring_h1.finish(put_ef(t1))
-    ring_h2.finish(put_ef(t2))
-
-    for tile, b in ((t1, c), (t2, 1 - c)):
+
+    def mix_start(k, tile):
         for half in range(2):
             block = tile[half]
             flipped = block.T
             for n in range(4):
                 for side in range(2):
                     at = n * 32 + side * 16
-                    mix[2 + side, half * 4 + n, b] = block[at : at + 16]
-                    mix[side, n * 2 + b, half] = flipped[at : at + 16]
-    mix_copies = [
-        remote(mix.at[lax.rem(x + d, 4)], mix_r.at[d - 1], mix_s.at[d - 1], mix_t.at[d - 1], on_x(d)) for d in (1, 2, 3)
-    ]
-    for copy in mix_copies:
-        copy.start()
-    for copy in mix_copies:
-        copy.wait_recv()
+                    mix[k, 2 + side, half * 4 + n] = block[at : at + 16]
+                    mix[k, side, n * 2 + half] = flipped[at : at + 16]
+        mix_b[k] = mix[k].astype(BF)
+        copies = []
+        for d in (1, 2, 3):
+            sems = mix_s.at[k, d - 1], mix_t.at[k, d - 1]
+            copies.append(remote(mix_b.at[k, lax.rem(x + d, 4)], mix_r.at[k, d - 1], *sems, on_x(d)))
+            copies[-1].start()
+        return copies
+
+    def mix_finish(k, copies):
+        b = c if k == 0 else 1 - c
+        for copy in copies:
+            copy.wait_recv()
+        for n in range(8):
+            total = mix[k, x, n] + mix_r[k, 0, n].astype(F32)
+            total = total + (mix_r[k, 1, n].astype(F32) + mix_r[k, 2, n].astype(F32))
+            summed[n * h + (n // 2 * 2 + b) * (1 - h), b * h + n % 2 * (1 - h)] = -0.5 * total
+
+    ring_h1.finish(put_ef(t1))
+    mix_copies = mix_start(0, t1)
+    ring_h2.step(6)
+    ring_h2.finish(put_ef(t2))
+    mix_2 = mix_start(1, t2)
+    mix_finish(0, mix_copies)
+    mix_finish(1, mix_2)
+    mix_copies += mix_2
     mine = z * h + (y * 2 + c) * (1 - h)
-    for n in range(8):
-        summed[n] = -0.5 * ((mix[x, n] + mix_r[0, n]) + (mix_r[1, n] + mix_r[2, n]))
     pieces[mine] = summed[mine]
 
     def piece_copy(d):
@@ -329,42 +390,48 @@
 
     for ring in (ring_dy, ring_dz, ring_e1, ring_e2, ring_qz, ring_qy, ring_h1, ring_h2):
         ring.drain()
-    for copy in x_copies + [mate_copy, mate_got_copy] + ef_copies + mix_copies + piece_copies:
+    for copy in x_copies + [mate_copy, mate_got_copy] + ef_copies + mix_copies + piece_copies + dgy_copies + dgz_copies:
         copy.wait_send()
 
 
 def shards(half_ints):
-    x = jnp.pad(half_ints, ((0, 0), (0, K // 3 - half_ints.shape[1]), (0, 0))).reshape(K, W)
     dma = pltpu.SemaphoreType.DMA
     bufs = [
         ((NY, 2, 4, 32, W), BF), ((NZ, 2, 2, 32, W), BF), ((NZ, 2, 2, 256, 128), BF), ((NY, 2, 4, 256, 128), BF),
-        ((NZ, 2, 1, 16, W), F32), ((NY, 2, 1, 16, W), F32), ((NY, 2, 1, 128, 128), F32), ((NZ, 2, 1, 128, 128), F32),
+        ((NZ, 2, 1, 16, W), BF), ((NY, 2, 1, 16, W), BF), ((NY, 2, 1, 128, 128), BF), ((NZ, 2, 1, 128, 128), BF),
     ]
     recvs = [((2, shape[0] - 1) + shape[2:], dtype) for shape, dtype in bufs]
-    scratch = [pltpu.VMEM((K, W), BF), pltpu.VMEM((2, KH, W), BF), pltpu.VMEM((KH, W), BF)]
+    scratch = [pltpu.VMEM((3, OCC, W), BF), pltpu.VMEM((K, W), BF)]
+    scratch += [pltpu.VMEM((K, W), BF), pltpu.VMEM((2, KH, W), BF), pltpu.VMEM((KH, W), BF)]
     scratch += [pltpu.VMEM(shape, dtype) for shape, dtype in bufs + recvs]
     scratch += [pltpu.VMEM((2, 16, W), F32)] * 3
     scratch += [pltpu.VMEM((2, 128, 128), F32)] * 2
     scratch += [
-        pltpu.VMEM((4, 8, 2, 16, 128), F32),
-        pltpu.VMEM((3, 8, 2, 16, 128), F32),
+        pltpu.VMEM((2, 4, 8, 16, 128), F32),
+        pltpu.VMEM((2, 4, 8, 16, 128), BF),
+        pltpu.VMEM((2, 3, 8, 16, 128), BF),
         pltpu.VMEM((8, 2, 16, 128), F32),
         pltpu.VMEM((8, 2, 16, 128), F32),
+        pltpu.VMEM((1, W), F32),
+        pltpu.VMEM((1, W), F32),
+        pltpu.VMEM((NY - 1, 1, W), F32),
+        pltpu.VMEM((NZ - 1, 1, W), F32),
     ]
     for shape, _ in bufs:
         scratch += [dma((2, shape[0] - 1))] * 2
-    scratch += [dma((2,))] * 6 + [dma((3,))] * 2 + [dma((7,))] * 2
+    scratch += [dma((3,))] + [dma((2,))] * 6 + [dma((2, 3))] * 2 + [dma((7,))] * 2
+    scratch += [dma((NY - 1,))] * 2 + [dma((NZ - 1,))] * 2
     out = pl.pallas_call(
         kernel,
         out_shape=jax.ShapeDtypeStruct((4, 16, W), F32),
-        in_specs=[pl.BlockSpec(memory_space=pltpu.VMEM)],
+        in_specs=[pl.BlockSpec(memory_space=pl.ANY)],
         out_specs=pl.BlockSpec(memory_space=pltpu.VMEM),
         scratch_shapes=scratch,
         compiler_params=pltpu.CompilerParams(
             collective_id=0, has_side_effects=True, vmem_limit_bytes=56 * 1024 * 1024
         ),
         cost_estimate=pl.CostEstimate(flops=2 * 1024 * 1024 * K * 3, bytes_accessed=4 << 20, transcendentals=0),
-    )(x)
+    )(half_ints)
     return out.transpose(1, 0, 2)
 
 

time: 112 us -> 103 us (0.920)
  Pallas kernels: 106 us -> 101 us
  local copies, waits for them, and re-layouts: 5.8 us -> 1.82 us
    pallas_call x1, Pallas kernels: 106 us -> 101 us  [shards(): pl.pallas_call(kernel, out_shape=jax.ShapeDtypeStruct((4, 16, W), F32), i...]
    pad x1 -> x0, local copies, waits for them, and re-layouts: 3.97 us -> none  [shards(): jnp.pad(half_ints, ((0, 0), (0, K // 3 - half_ints.shape[1]), (0, 0)))]
where the time goes in v2:
time: 103 us
  Pallas kernels  101 us (98%)
  local copies, waits for them, and re-layouts  1.82 us (2%)
    pallas_call x1, Pallas kernels, shards(): pl.pallas_call(kernel, out_shape=jax.ShapeDtypeStruct((4, 16, W), F32), i...  101 us

profile of v2, /device:TPU:1, one launch (start us, length us, event | category | flops | bytes accessed | tf_op | source)
XLA Modules:
  0.0 102.8 jit_solution(14791398596895715577)
XLA Ops:
  0.0 101.0 %shard_map.17 = f32[4,16,1024]{2,1,0:T(8,128)} custom-call(bf16[3,500,1024]{2,1,0:T(8,128)(2,1)} %half_ints.1), custom_call_target="tpu_custom_call" | custom-call | flops 9663676416 | bytes 4194304 | tf_op jit(solution)/shard_map/pallas_call | solution.py:424
  101.0 1.8 %copy.2 = f32[16,4,1024]{2,1,0:T(4,128)} copy(f32[16,4,1024]{2,0,1:T(8,128)} %bitcast.1) | data formatting | bytes 524288 | tf_op jit(solution)/shard_map/transpose | solution.py:435

commit v3 on v1

v3 whole, which is shorter than its diff:
```python
import functools

import jax
import jax.numpy as jnp
from jax import lax
from jax.experimental import pallas as pl
from jax.experimental.pallas import tpu as pltpu
from jax.sharding import PartitionSpec as P

MESH = pl.DeviceIdType.MESH
BF = jnp.bfloat16
F32 = jnp.float32
NZ, NY = 8, 4
W = 1024
K = 1536
KH = K // 2
ORDER = (4, 3, 5, 2, 6, 1, 7, 0)
PARTS = 4
OCC = 500


class Ring:
    def __init__(self, size, pos, device_at, buf, recv, send_sem, recv_sem):
        self.size, self.pos, self.buf, self.recv = size, pos, buf, recv
        self.peers = (device_at(lax.rem(pos + 1, size)), device_at(lax.rem(pos + size - 1, size)))
        self.send_sem, self.recv_sem = send_sem, recv_sem
        self.m, self.rows, self.lanes = buf.shape[2:]

    def where(self, direction, i):
        distance = self.size // 2 - (i + 1) // 2
        half = (i + direction) % 2
        chunk = lax.rem(self.pos + (distance if direction == 0 else self.size - distance), self.size)
        return chunk, half

    def copy(self, direction, i):
        chunk, half = self.where(direction, i)
        return pltpu.make_async_remote_copy(
            src_ref=self.buf.at[chunk, half],
            dst_ref=self.recv.at[direction, i],
            send_sem=self.send_sem.at[direction, i],
            recv_sem=self.recv_sem.at[direction, i],
            device_id=self.peers[direction],
            device_id_type=MESH,
        )

    def step(self, i):
        for direction in range(2):
            if i >= 2:
                self.copy(direction, i - 2).wait_recv()
                chunk, half = self.where(direction, i)
                self.add(chunk, half, direction, i - 2)
            self.copy(direction, i).start()

    def add(self, chunk, half, direction, i):
        rows = min(self.rows, 32 if self.lanes == W else 128)
        parts = self.rows // rows

        def body(t, _):
            a, b = t // parts, pl.multiple_of((t % parts) * rows, rows)
            at = (chunk, half, a, pl.ds(b, rows))
            total = self.buf[at].astype(F32) + self.recv[direction, i, a, pl.ds(b, rows)].astype(F32)
            self.buf[at] = total.astype(self.buf.dtype)
            return _

        lax.fori_loop(0, self.m * parts, body, 0)

    def finish(self, put, sides=1):
        last = self.size - 2
        for direction in range(2):
            self.copy(direction, last - 1).wait_recv()
            self.copy(direction, last).wait_recv()
        for half in range(2):
            up, down = (last, last - 1) if half == 0 else (last - 1, last)

            def body(t, _, half=half, up=up, down=down):
                a, side = t // sides, t % sides
                rows = self.rows // sides
                r = pl.ds(pl.multiple_of(side * rows, rows), rows)
                total = (
                    self.buf[self.pos, half, a, r].astype(F32)
                    + self.recv[0, up, a, r].astype(F32)
                    + self.recv[1, down, a, r].astype(F32)
                )
                put(half * self.m + a, side, total)
                return _

            lax.fori_loop(0, self.m * sides, body, 0)

    def drain(self):
        for direction in range(2):
            for i in range(self.size - 1):
                self.copy(direction, i).wait_send()


def gram_tiles(lhs, rhs, put):
    def body(t, _):
        i, j = t // 2, t % 2
        left = lhs[:, pl.ds(pl.multiple_of(i * 256, 256), 256)]
        right = rhs[:, pl.ds(pl.multiple_of(j * 512, 512), 512)]
        tile = lax.dot_general(left, right, (((0,), (0,)), ((), ())), preferred_element_type=F32)
        put(i, j, tile)
        return _

    lax.fori_loop(0, 8, body, 0)


def kernel(
    half_ints, out_ref, raw, x_ref, mate_x, got, mate_got, left,
    da, db, ea, eb, q0, q1, q2, q3,
    da_r, db_r, ea_r, eb_r, q0_r, q1_r, q2_r, q3_r,
    fa, fb, f_r, tile_y, tile_y_r, tile, mix, mix_r, summed, pieces, diag, diag_sum, diag_y, diag_z,
    da_s, da_t, db_s, db_t, ea_s, ea_t, eb_s, eb_t, q0_s, q0_t, q1_s, q1_t, q2_s, q2_t, q3_s, q3_t,
    raw_t, x_s, x_t, mate_s, mate_t, f_s, f_t, ty_s, ty_t, mix_s, mix_t, piece_s, piece_t, dgy_s, dgy_t, dgz_s, dgz_t,
):
    raw_copies = [pltpu.make_async_copy(half_ints.at[p], raw.at[p], raw_t.at[p]) for p in range(3)]
    for copy in raw_copies:
        copy.start()
    a = lax.axis_index("aux")
    r = lax.axis_index("rows")
    z, y, l = a // 8, (a // 2) % 4, a % 2
    h, c = r // 2, r % 2
    x = 2 * h + l

    def dev(x_, y_, z_, c_):
        return (z_ * 8 + y_ * 2 + x_ % 2, 2 * (x_ // 2) + c_)

    def on_x(step):
        return dev(lax.rem(x + step, 4), y, z, c)

    def on_y(step):
        return dev(x, lax.rem(y + step, NY), z, c)

    def on_z(step):
        return dev(x, y, lax.rem(z + step, NZ), c)

    mate = dev(x, y, z, 1 - c)

    barrier = pltpu.get_barrier_semaphore()
    partners = [mate, on_x(1), on_x(3), on_y(1), on_y(3), on_z(1), on_z(7)]
    for partner in partners:
        pl.semaphore_signal(barrier, inc=1, device_id=partner, device_id_type=MESH)
    whole = OCC // 16 * 16
    for p in range(3):
        raw_copies[p].wait()

        def body(t, _, p=p):
            rows = pl.multiple_of(t * 16, 16)
            x_ref[pl.ds(p * 512 + rows, 16), :] = raw[p, pl.ds(rows, 16), :]
            return _

        lax.fori_loop(0, whole // 16, body, 0)
        tail = jnp.zeros((512 - OCC, W), BF)
        x_ref[p * 512 + whole : p * 512 + 512, :] = jnp.concatenate([raw[p, whole:OCC, :], tail], axis=0)
    pl.semaphore_wait(barrier, len(partners))

    def remote(src, dst, send, recv, device):
        return pltpu.make_async_remote_copy(
            src_ref=src, dst_ref=dst, send_sem=send, recv_sem=recv, device_id=device, device_id_type=MESH
        )

    def columns_of(h_, k):
        block = h_ * lax.rem(z + ORDER[k], NZ) + (1 - h_) * k
        return pl.ds(pl.multiple_of(block * 128, 128), 128)

    def x_copy(k, n, step):
        target_h = lax.rem(x + step, 4) // 2
        rows = pl.ds(pl.multiple_of(target_h * KH, KH), KH)
        columns = columns_of(h, k)
        return remote(x_ref.at[rows, columns], got.at[h, :, columns], x_s.at[n, k], x_t.at[h, k], on_x(step))

    def x_wait(slot, *ks):
        for k in ks:
            columns = columns_of(slot, k)
            remote(x_ref.at[pl.ds(0, KH), columns], got.at[slot, :, columns], x_s.at[0, k], x_t.at[slot, k], mate).wait_recv()

    x_copies = [x_copy(k, n, step) for k in range(NZ) for n, step in enumerate((1, 3))]
    for copy in x_copies:
        copy.start()
    mate_copy = remote(x_ref, mate_x, mate_s.at[PARTS], mate_t.at[PARTS], mate)
    mate_copy.start()

    def z_ring(*refs):
        return Ring(NZ, z, lambda p: dev(x, y, p, c), *refs)

    def y_ring(*refs):
        return Ring(NY, y, lambda p: dev(x, p, z, c), *refs)

    ring_a = y_ring(da, da_r, da_s, da_t)
    ring_b = y_ring(db, db_r, db_s, db_t)
    ring_ea = z_ring(ea, ea_r, ea_s, ea_t)
    ring_eb = z_ring(eb, eb_r, eb_s, eb_t)
    rings = [
        z_ring(q0, q0_r, q0_s, q0_t),
        z_ring(q1, q1_r, q1_s, q1_t),
        z_ring(q2, q2_r, q2_s, q2_t),
        z_ring(q3, q3_r, q3_s, q3_t),
    ]

    def put_rows(ref, i, j, tile_):
        tile_ = tile_.astype(BF)
        for k in range(2):
            zi = 2 * i + k
            for yi in range(4):
                rows = tile_[k * 128 + yi * 32 : k * 128 + yi * 32 + 32]
                ref[yi, zi // 4, zi % 4, :, pl.ds(pl.multiple_of(j * 512, 512), 512)] = rows

    def put_a(i, j, tile_):
        on_diagonal = lax.broadcasted_iota(jnp.int32, (256, 512), 1) - lax.broadcasted_iota(jnp.int32, (256, 512), 0)
        on_diagonal = on_diagonal == i * 256 - j * 512
        columns = pl.ds(pl.multiple_of(j * 512, 512), 512)
        diag[:, columns] += jnp.sum(jnp.where(on_diagonal, tile_, 0.0), axis=0, keepdims=True)
        put_rows(da, i, j, jnp.where(on_diagonal, 0.0, tile_))

    def put_b(i, j, tile_):
        put_rows(db, i, j, tile_)

    def put_ea(n, side, total):
        ea[n, side, 0] = total.astype(BF)

    def put_eb(n, side, total):
        eb[n, side, 0] = total.astype(BF)

    def put_f(ref):
        def put(half, part, total):
            ref[half] = total

        return put

    def mate_part(p):
        columns = pl.ds(p * 256, 256)
        return remote(got.at[0, :, columns], mate_got.at[:, columns], mate_s.at[p], mate_t.at[p], mate)

    def turn(p, which):
        rows = (mate_got[:, p * 256 : p * 256 + 256] if which else got[0, :, p * 256 : p * 256 + 256]).T
        for yi in range(4):
            for k in range(2):
                at = which * 256 + yi * 64 + k * 32
                left[p, at : at + 32, :] = rows[k * 128 + yi * 32 : k * 128 + yi * 32 + 32]

    def cross(p, *ks):
        for k in ks:
            block = lax.rem(z + ORDER[k], NZ)
            right = got[1, :, pl.ds(pl.multiple_of(block * 128, 128), 128)]
            product = lax.dot_general(left[p], right, (((1,), (0,)), ((), ())), preferred_element_type=F32).astype(BF)
            for which in range(2):
                rings[p].buf[block, which, 0] = product[which * 256 : which * 256 + 256]

    def over_y(p):
        def put(which, yi, total):
            tile_y[p, yi, which] = total.astype(BF)

        rings[p].finish(put, 4)
        copies = []
        for d in range(1, NY):
            sems = ty_s.at[p, d - 1], ty_t.at[p, d - 1]
            copies.append(remote(tile_y.at[p, lax.rem(y + d, NY)], tile_y_r.at[p, d - 1], *sems, on_y(d)))
            copies[-1].start()
        return copies

    def over_x(p, copies):
        for copy in copies:
            copy.wait_recv()
        for which in range(2):
            total = tile_y[p, y, which].astype(F32)
            for d in range(NY - 1):
                total = total + tile_y_r[p, d, which].astype(F32)
            tile[p, c if which == 0 else 1 - c] = total
        flipped = jnp.concatenate([tile[p, 0], tile[p, 1]], axis=0).T
        for side in range(2):
            for n in range(4):
                at = (n % 2) * 32 + side * 16
                mix[p, 2 + side, n] = tile[p, n // 2, at : at + 16, :]
                at = n * 32 + side * 16
                mix[p, side, n] = flipped[at : at + 16]
        out = []
        for d in (1, 2, 3):
            sems = mix_s.at[p, d - 1], mix_t.at[p, d - 1]
            out.append(remote(mix.at[p, lax.rem(x + d, 4)], mix_r.at[p, d - 1], *sems, on_x(d)))
            out[-1].start()
        return out

    def collect(p, copies):
        for copy in copies:
            copy.wait_recv()
        for n in range(4):
            total = -0.5 * ((mix[p, x, n] + mix_r[p, 0, n]) + (mix_r[p, 1, n] + mix_r[p, 2, n]))

            @pl.when(h == 1)
            def _(total=total, n=n):
                summed[2 * p + n % 2, n // 2] = total

            @pl.when(h == 0)
            def _(total=total, n=n):
                at = (p % 2) * 64
                for b in range(2):
                    summed[n * 2 + b, p // 2, :, at : at + 64] = total[:, b * 64 : b * 64 + 64]

    started = [mate_copy]

    def send_part(p):
        copy = mate_part(p)
        copy.start()
        started.append(copy)
        return copy

    diag[...] = jnp.zeros_like(diag)
    gram_tiles(x_ref, x_ref, put_a)
    ring_a.step(0)
    ring_a.step(1)
    mate_copy.wait_recv()
    gram_tiles(mate_x, x_ref, put_b)
    x_wait(0, 0, 1)
    part = send_part(0)
    turn(0, 0)
    ring_a.step(2)
    ring_b.step(0)
    ring_b.step(1)
    x_wait(1, 0, 1, 2)
    part.wait_recv()
    turn(0, 1)
    cross(0, 0, 1, 2)
    rings[0].step(0)
    rings[0].step(1)
    x_wait(0, 2, 3)
    part = send_part(1)
    turn(1, 0)
    rings[0].step(2)
    x_wait(1, 3, 4)
    cross(0, 3, 4)
    rings[0].step(3)
    part.wait_recv()
    turn(1, 1)
    cross(1, 0, 1, 2, 3, 4)
    rings[1].step(0)
    rings[1].step(1)
    ring_a.finish(put_ea, 2)
    dgy_copies = [remote(diag, diag_y.at[d - 1], dgy_s.at[d - 1], dgy_t.at[d - 1], on_y(d)) for d in range(1, NY)]
    for copy in dgy_copies:
        copy.start()
    ring_ea.step(0)
    ring_ea.step(1)
    rings[0].step(4)
    rings[1].step(2)
    x_wait(0, 4, 5)
    part = send_part(2)
    turn(2, 0)
    ring_b.step(2)
    rings[1].step(3)
    part.wait_recv()
    turn(2, 1)
    cross(2, 0, 1, 2, 3, 4)
    rings[2].step(0)
    rings[2].step(1)
    ring_ea.step(2)
    ring_ea.step(3)
    rings[1].step(4)
    rings[2].step(2)
    x_wait(1, 5, 6)
    cross(0, 5, 6)
    rings[0].step(5)
    cross(1, 5, 6)
    rings[1].step(5)
    cross(2, 5, 6)
    rings[0].step(6)
    ring_ea.step(4)
    ring_ea.step(5)
    rings[2].step(3)
    rings[1].step(6)
    x_wait(0, 6, 7)
    part = send_part(3)
    turn(3, 0)
    x_wait(1, 7)
    cross(0, 7)
    cross(1, 7)
    cross(2, 7)
    part.wait_recv()
    turn(3, 1)
    cross(3, *range(8))
    rings[3].step(0)
    rings[3].step(1)
    rings[2].step(4)
    y0 = over_y(0)
    rings[2].step(5)
    rings[3].step(2)
    y1 = over_y(1)
    rings[3].step(3)
    rings[2].step(6)
    ring_ea.step(6)
    ring_b.finish(put_eb, 2)
    ring_eb.step(0)
    ring_eb.step(1)
    for copy in dgy_copies:
        copy.wait_recv()
    diag_sum[...] = (diag[...] + diag_y[0]) + (diag_y[1] + diag_y[2])
    dgz_copies = [remote(diag_sum, diag_z.at[d - 1], dgz_s.at[d - 1], dgz_t.at[d - 1], on_z(d)) for d in range(1, NZ)]
    for copy in dgz_copies:
        copy.start()
    rings[3].step(4)
    x0 = over_x(0, y0)
    ring_eb.step(2)
    rings[3].step(5)
    x1 = over_x(1, y1)
    y2 = over_y(2)
    ring_eb.step(3)
    ring_ea.finish(put_f(fa))
    rings[3].step(6)
    ring_eb.step(4)
    collect(0, x0)
    collect(1, x1)
    ring_eb.step(5)
    x2 = over_x(2, y2)
    y3 = over_y(3)
    ring_eb.step(6)
    collect(2, x2)
    x3 = over_x(3, y3)
    ring_eb.finish(put_f(fb))
    for copy in dgz_copies:
        copy.wait_recv()
    total_diag = diag_sum[...]
    for d in range(NZ - 1):
        total_diag = total_diag + diag_z[d]
    for side in range(2):
        row = lax.broadcasted_iota(jnp.int32, (16, W), 0) + (z * 128 + y * 32 + side * 16)
        own = lax.broadcasted_iota(jnp.int32, (16, W), 1) == row
        fa[side] += jnp.where(own, total_diag, 0.0)

    near = dev(2 * h + (1 - l), y, z, c)
    f_copies = [remote(ref.at[1 - l], f_r.at[k], f_s.at[k], f_t.at[k], near) for k, ref in enumerate((fa, fb))]
    for copy in f_copies:
        copy.start()
    collect(3, x3)

    mine = z * h + (y * 2 + c) * (1 - h)

    def piece_copy(d):
        n = lax.rem(mine + d, 8)
        target = dev(x, y * h + (n // 2) * (1 - h), n * h + z * (1 - h), c * h + (n % 2) * (1 - h))
        return remote(summed.at[n], pieces.at[mine], piece_s.at[d - 1], piece_t.at[d - 1], target)

    piece_copies = [piece_copy(d) for d in range(1, 8)]
    for copy in piece_copies:
        copy.start()
    pieces[mine] = summed[mine]
    for k, ref in enumerate((fa, fb)):
        f_copies[k].wait_recv()
        block = 2 * h + (c if k == 0 else 1 - c)
        out_ref[block] = -0.5 * (ref[l] + f_r[k])
    for copy in piece_copies:
        copy.wait_recv()

    @pl.when(h == 1)
    def _():
        for s in range(2):
            for n in range(8):
                out_ref[s, :, n * 128 : n * 128 + 128] = pieces[n, s]

    @pl.when(h == 0)
    def _():
        for s in range(2):
            for n in range(8):
                at = (n % 4) * 32
                parts = [pieces[v * 2 + s, n // 4][:, at : at + 32] for v in range(4)]
                out_ref[2 + s, :, n * 128 : n * 128 + 128] = jnp.concatenate(parts, axis=1)

    for ring in [ring_a, ring_b, ring_ea, ring_eb] + rings:
        ring.drain()
    for copy in x_copies + started + y0 + y1 + y2 + y3 + x0 + x1 + x2 + x3:
        copy.wait_send()
    for copy in f_copies + piece_copies + dgy_copies + dgz_copies:
        copy.wait_send()


def shards(half_ints):
    dma = pltpu.SemaphoreType.DMA
    vmem = pltpu.VMEM
    bufs = [(NY, 2, 4, 32, W)] * 2 + [(NZ, 2, 1, 16, W)] * 2 + [(NZ, 2, 1, 256, 128)] * PARTS
    scratch = [vmem((3, OCC, W), BF), vmem((K, W), BF), vmem((K, W), BF)]
    scratch += [vmem((2, KH, W), BF), vmem((KH, W), BF), vmem((PARTS, 512, KH), BF)]
    scratch += [vmem(shape, BF) for shape in bufs]
    scratch += [vmem((2, shape[0] - 1) + shape[2:], BF) for shape in bufs]
    scratch += [vmem((2, 16, W), F32)] * 3
    scratch += [
        vmem((PARTS, NY, 2, 64, 128), BF),
        vmem((PARTS, NY - 1, 2, 64, 128), BF),
        vmem((PARTS, 2, 64, 128), F32),
        vmem((PARTS, 4, 4, 16, 128), F32),
        vmem((PARTS, 3, 4, 16, 128), F32),
        vmem((8, 2, 16, 128), F32),
        vmem((8, 2, 16, 128), F32),
        vmem((1, W), F32),
        vmem((1, W), F32),
        vmem((NY - 1, 1, W), F32),
        vmem((NZ - 1, 1, W), F32),
    ]
    for shape in bufs:
        scratch += [dma((2, shape[0] - 1))] * 2
    scratch += [dma((3,))] + [dma((2, NZ))] * 2 + [dma((PARTS + 1,))] * 2 + [dma((2,))] * 2
    scratch += [dma((PARTS, NY - 1))] * 2 + [dma((PARTS, 3))] * 2 + [dma((7,))] * 2
    scratch += [dma((NY - 1,))] * 2 + [dma((NZ - 1,))] * 2
    out = pl.pallas_call(
        kernel,
        out_shape=jax.ShapeDtypeStruct((4, 16, W), F32),
        in_specs=[pl.BlockSpec(memory_space=pl.ANY)],
        out_specs=pl.BlockSpec(memory_space=pltpu.VMEM),
        scratch_shapes=scratch,
        compiler_params=pltpu.CompilerParams(
            collective_id=0, has_side_effects=True, vmem_limit_bytes=56 * 1024 * 1024
        ),
        cost_estimate=pl.CostEstimate(flops=2 * 1024 * 1024 * K * 3, bytes_accessed=4 << 20, transcendentals=0),
    )(half_ints)
    return out.transpose(1, 0, 2)


def solution(mesh):
    placed = (P("aux", None, "rows"),)
    return jax.shard_map(
        shards, mesh=mesh, in_specs=placed, out_specs=P("aux", None, "rows"), check_vma=False
    )
```

time: 112 us -> 98 us (0.88)
  Pallas kernels: 106 us -> 96.1 us
  local copies, waits for them, and re-layouts: 5.8 us -> 1.82 us
    pallas_call x1, Pallas kernels: 106 us -> 96.1 us  [shards(): pl.pallas_call(kernel, out_shape=jax.ShapeDtypeStruct((4, 16, W), F32), i...]
    pad x1 -> x0, local copies, waits for them, and re-layouts: 3.97 us -> none  [shards(): jnp.pad(half_ints, ((0, 0), (0, K // 3 - half_ints.shape[1]), (0, 0)))]
where the time goes in v3:
time: 98 us; the launch traced here: 97.9 us
  Pallas kernels  96.1 us (98%)
  local copies, waits for them, and re-layouts  1.82 us (2%)
    pallas_call x1, Pallas kernels, shards(): pl.pallas_call(kernel, out_shape=jax.ShapeDtypeStruct((4, 16, W), F32), i...  96.1 us

profile of v3, /device:TPU:1, one launch (start us, length us, event | category | flops | bytes accessed | tf_op | source)
XLA Modules:
  0.0 97.9 jit_solution(162741904749440245)
XLA Ops:
  0.0 96.1 %shard_map.17 = f32[4,16,1024]{2,1,0:T(8,128)} custom-call(bf16[3,500,1024]{2,1,0:T(8,128)(2,1)} %half_ints.1), custom_call_target="tpu_custom_call" | custom-call | flops 9663676416 | bytes 4194304 | tf_op jit(solution)/shard_map/pallas_call | solution.py:500
  96.1 1.8 %copy.2 = f32[16,4,1024]{2,1,0:T(4,128)} copy(f32[16,4,1024]{2,0,1:T(8,128)} %bitcast.1) | data formatting | bytes 524288 | tf_op jit(solution)/shard_map/transpose | solution.py:511

commit v4 on v3

v4 whole, which is shorter than its diff:
```python
import functools

import jax
import jax.numpy as jnp
from jax import lax
from jax.experimental import pallas as pl
from jax.experimental.pallas import tpu as pltpu
from jax.sharding import PartitionSpec as P

MESH = pl.DeviceIdType.MESH
BF = jnp.bfloat16
F32 = jnp.float32
NZ, NY = 8, 4
W = 1024
K = 1536
KH = K // 2
ORDER = (4, 3, 5, 2, 6, 1, 7, 0)
PARTS = 4
SPLIT = 5
GROUPS = ((7,), (5, 6), (3, 4), (1, 2), (0,))
SCHEDULE = (
    "gC", "gA", "A.0", "A.1", "C.0", "C.1", "gB0", "gB1", "sp0", "A.2", "tu0.0", "C.2", "C.3", "B.0", "B.1", "tu0.1",
    "cr0.3", "cr0.4", "R0.0", "R0.1", "C.4", "Af", "C.5", "sp1", "tu1.0", "R0.2", "tu1.1", "C.6", "cr0.2", "R0.3",
    "ca1", "V1.0", "B.2", "V1.1", "R0.4", "Cf", "fcs", "sp2", "tu2.0", "tu2.1", "cr2.4", "R2.0", "cr2.3", "R2.1",
    "cr2.2", "V1.2", "sp3", "cr0.1", "R0.5", "tu3.0", "cr2.1", "R0.6", "tu3.1", "cr3.1", "cr3.4", "R3.0", "R2.2",
    "cr3.3", "R3.1", "cr3.2", "R2.3", "cr0.0", "sp4", "cb1", "W1.0", "W1.1", "Bf", "Ex", "tu4.0", "Y0", "tu4.1",
    "cr2.0", "R3.2", "c4.0", "c4.1", "Q.0", "dgy", "R2.4", "Q.1", "cr3.0", "R3.3", "V1f", "R1.0", "R1.1", "R2.5",
    "W1.2", "R3.4", "R2.6", "X0", "R1.2", "R3.5", "R1.3", "Q.2", "dgz", "R3.6", "W1f", "Ea", "R1.4", "E.0", "Y2",
    "Qf", "R1.5", "E.1", "K0", "G", "Y3", "R1.6", "E.2", "X2", "X3", "E.3", "Y1", "X1", "E.4", "K2", "E.5", "K3",
    "E.6", "K1", "pieces", "Ef", "out",
)
FROM = (0, 256, 512, 768, 896, 1024)
OCC = 500


class Ring:
    def __init__(self, size, pos, device_at, buf, recv, send_sem, recv_sem):
        self.size, self.pos, self.buf, self.recv = size, pos, buf, recv
        self.peers = (device_at(lax.rem(pos + 1, size)), device_at(lax.rem(pos + size - 1, size)))
        self.send_sem, self.recv_sem = send_sem, recv_sem
        self.m, self.rows, self.lanes = buf.shape[2:]

    def where(self, direction, i):
        distance = self.size // 2 - (i + 1) // 2
        half = (i + direction) % 2
        chunk = lax.rem(self.pos + (distance if direction == 0 else self.size - distance), self.size)
        return chunk, half

    def copy(self, direction, i):
        chunk, half = self.where(direction, i)
        return pltpu.make_async_remote_copy(
            src_ref=self.buf.at[chunk, half],
            dst_ref=self.recv.at[direction, i],
            send_sem=self.send_sem.at[direction, i],
            recv_sem=self.recv_sem.at[direction, i],
            device_id=self.peers[direction],
            device_id_type=MESH,
        )

    def step(self, i):
        for direction in range(2):
            if i >= 2:
                self.copy(direction, i - 2).wait_recv()
                chunk, half = self.where(direction, i)
                self.add(chunk, half, direction, i - 2)
            self.copy(direction, i).start()

    def add(self, chunk, half, direction, i):
        rows = min(self.rows, 32 if self.lanes == W else 128)
        parts = self.rows // rows

        def body(t, _):
            a, b = t // parts, pl.multiple_of((t % parts) * rows, rows)
            at = (chunk, half, a, pl.ds(b, rows))
            total = self.buf[at].astype(F32) + self.recv[direction, i, a, pl.ds(b, rows)].astype(F32)
            self.buf[at] = total.astype(self.buf.dtype)
            return _

        lax.fori_loop(0, self.m * parts, body, 0)

    def finish(self, put, sides=1):
        last = self.size - 2
        for direction in range(2):
            self.copy(direction, last - 1).wait_recv()
            self.copy(direction, last).wait_recv()
        for half in range(2):
            up, down = (last, last - 1) if half == 0 else (last - 1, last)

            def body(t, _, half=half, up=up, down=down):
                a, side = t // sides, t % sides
                rows = self.rows // sides
                r = pl.ds(pl.multiple_of(side * rows, rows), rows)
                total = (
                    self.buf[self.pos, half, a, r].astype(F32)
                    + self.recv[0, up, a, r].astype(F32)
                    + self.recv[1, down, a, r].astype(F32)
                )
                put(half * self.m + a, side, total)
                return _

            lax.fori_loop(0, self.m * sides, body, 0)

    def drain(self):
        for direction in range(2):
            for i in range(self.size - 1):
                self.copy(direction, i).wait_send()


def gram_tiles(lhs, rhs, j, put):
    def body(i, _):
        left = lhs[:, pl.ds(pl.multiple_of(i * 256, 256), 256)]
        right = rhs[:, j * 512 : j * 512 + 512]
        tile = lax.dot_general(left, right, (((0,), (0,)), ((), ())), preferred_element_type=F32)
        put(i, tile)
        return _

    lax.fori_loop(0, 4, body, 0)


def kernel(
    half_ints, out_ref, raw, x_ref, mate_x, got, mate_got, left, left_4,
    da, db, dc, e, q0, q1, q2, q3, q4, v1, w1,
    da_r, db_r, dc_r, e_r, q0_r, q1_r, q2_r, q3_r, q4_r, v1_r, w1_r,
    e_own, e_near, e_sum, fc, fc_r, gc, gc_r, h4, h4_r,
    tile_y, tile_y_r, tile, mix, mix_r, summed, pieces, diag, diag_sum, diag_y, diag_z, diag_x,
    da_s, da_t, db_s, db_t, dc_s, dc_t, e_s, e_t, q0_s, q0_t, q1_s, q1_t, q2_s, q2_t, q3_s, q3_t, q4_s, q4_t, v1_s, v1_t, w1_s, w1_t,
    raw_t, x_s, x_t, mate_s, mate_t, near_s, near_t, ty_s, ty_t, mix_s, mix_t, piece_s, piece_t,
    dgy_s, dgy_t, dgz_s, dgz_t, fc_s, fc_t, h4_s, h4_t,
):
    raw_copies = [pltpu.make_async_copy(half_ints.at[p], raw.at[p], raw_t.at[p]) for p in range(3)]
    for copy in raw_copies:
        copy.start()
    a = lax.axis_index("aux")
    r = lax.axis_index("rows")
    z, y, l = a // 8, (a // 2) % 4, a % 2
    h, c = r // 2, r % 2
    x = 2 * h + l

    def dev(x_, y_, z_, c_):
        return (z_ * 8 + y_ * 2 + x_ % 2, 2 * (x_ // 2) + c_)

    def on_x(step):
        return dev(lax.rem(x + step, 4), y, z, c)

    def on_y(step):
        return dev(x, lax.rem(y + step, NY), z, c)

    def on_z(step):
        return dev(x, y, lax.rem(z + step, NZ), c)

    mate = dev(x, y, z, 1 - c)

    barrier = pltpu.get_barrier_semaphore()
    partners = [mate, on_x(1), on_x(3), on_y(1), on_y(3), on_z(1), on_z(7)]
    for partner in partners:
        pl.semaphore_signal(barrier, inc=1, device_id=partner, device_id_type=MESH)
    whole = OCC // 16 * 16
    for p in range(3):
        raw_copies[p].wait()

        def body(t, _, p=p):
            rows = pl.multiple_of(t * 16, 16)
            x_ref[pl.ds(p * 512 + rows, 16), :] = raw[p, pl.ds(rows, 16), :]
            return _

        lax.fori_loop(0, whole // 16, body, 0)
        tail = jnp.zeros((512 - OCC, W), BF)
        x_ref[p * 512 + whole : p * 512 + 512, :] = jnp.concatenate([raw[p, whole:OCC, :], tail], axis=0)
    pl.semaphore_wait(barrier, len(partners))

    def remote(src, dst, send, recv, device):
        return pltpu.make_async_remote_copy(
            src_ref=src, dst_ref=dst, send_sem=send, recv_sem=recv, device_id=device, device_id_type=MESH
        )

    def columns_of(h_, k):
        block = h_ * lax.rem(z + ORDER[k], NZ) + (1 - h_) * k
        return pl.ds(pl.multiple_of(block * 128, 128), 128)

    def x_copy(k, n, step):
        target_h = lax.rem(x + step, 4) // 2
        rows = pl.ds(pl.multiple_of(target_h * KH, KH), KH)
        columns = columns_of(h, k)
        return remote(x_ref.at[rows, columns], got.at[h, :, columns], x_s.at[n, k], x_t.at[h, k], on_x(step))

    arrived = set()

    def x_wait(slot, *ks):
        for k in ks:
            if (slot, k) in arrived:
                continue
            arrived.add((slot, k))
            columns = columns_of(slot, k)
            remote(x_ref.at[pl.ds(0, KH), columns], got.at[slot, :, columns], x_s.at[0, k], x_t.at[slot, k], mate).wait_recv()

    x_copies = [x_copy(k, n, step) for k in range(NZ) for n, step in enumerate((1, 3))]
    for copy in x_copies:
        copy.start()
    mate_copy = remote(x_ref, mate_x, mate_s.at[5], mate_t.at[5], mate)
    mate_copy.start()

    def z_ring(*refs):
        return Ring(NZ, z, lambda p: dev(x, y, p, c), *refs)

    def y_ring(*refs):
        return Ring(NY, y, lambda p: dev(x, p, z, c), *refs)

    ring_a = y_ring(da, da_r, da_s, da_t)
    ring_b = y_ring(db, db_r, db_s, db_t)
    ring_c = z_ring(dc, dc_r, dc_s, dc_t)
    ring_e = z_ring(e, e_r, e_s, e_t)
    rings = [
        z_ring(q0, q0_r, q0_s, q0_t),
        z_ring(q1, q1_r, q1_s, q1_t),
        z_ring(q2, q2_r, q2_s, q2_t),
        z_ring(q3, q3_r, q3_s, q3_t),
    ]
    ring_4 = y_ring(q4, q4_r, q4_s, q4_t)
    ring_v = y_ring(v1, v1_r, v1_s, v1_t)
    ring_w = y_ring(w1, w1_r, w1_s, w1_t)

    def no_diagonal(i, j, tile_):
        on_diagonal = lax.broadcasted_iota(jnp.int32, (256, 512), 1) - lax.broadcasted_iota(jnp.int32, (256, 512), 0)
        on_diagonal = on_diagonal == i * 256 - j * 512
        diag[:, j * 512 : j * 512 + 512] += jnp.sum(jnp.where(on_diagonal, tile_, 0.0), axis=0, keepdims=True)
        return jnp.where(on_diagonal, 0.0, tile_)

    def put_y(ref, columns, i, tile_):
        tile_ = tile_.astype(BF)
        for k in range(2):
            zi = 2 * i + k
            for yi in range(4):
                rows = tile_[k * 128 + yi * 32 : k * 128 + yi * 32 + 32]
                ref[yi, zi // 4, zi % 4, :, columns] = rows

    def put_a(i, tile_):
        put_y(da, slice(0, 512), i, no_diagonal(i, 1, tile_))

    def put_c(i, tile_):
        tile_ = no_diagonal(i, 0, tile_).astype(BF)
        for k in range(2):
            for yi in range(4):
                dc[2 * i + k, yi // 2, yi % 2] = tile_[k * 128 + yi * 32 : k * 128 + yi * 32 + 32]

    def put_ea(n, side, total):
        e_own[side, n, 0, :, 0:512] = total.astype(BF)

    def put_eb(n, side, total):
        e_own[side, n, 0, :, 512:768] = total[:, 0:256].astype(BF)
        e_own[side, n, 1] = total[:, 256:1024].astype(BF)

    def put_fc(n, side, total):
        fc[n] = total.astype(BF)

    def put_e(half, part, total):
        e_sum[half] = total

    def mate_part(p):
        columns = pl.ds(FROM[p], FROM[p + 1] - FROM[p])
        return remote(got.at[0, :, columns], mate_got.at[:, columns], mate_s.at[p], mate_t.at[p], mate)

    def turn(p, which):
        size = FROM[p + 1] - FROM[p]
        ref = left.at[p] if p < 3 else left_4.at[p - 3]
        columns = slice(FROM[p], FROM[p + 1])
        rows = (mate_got[:, columns] if which else got[0, :, columns]).T
        for yi in range(4):
            for k in range(size // 128):
                at = which * size + yi * (size // 4) + k * 32
                ref[at : at + 32, :] = rows[k * 128 + yi * 32 : k * 128 + yi * 32 + 32]

    def cross(p, *ks):
        size = FROM[p + 1] - FROM[p]
        for k in ks:
            block = lax.rem(z + ORDER[k], NZ)
            right = got[1, :, pl.ds(pl.multiple_of(block * 128, 128), 128)]
            rows = left[p] if p < 3 else left_4[p - 3]
            product = lax.dot_general(rows, right, (((1,), (0,)), ((), ())), preferred_element_type=F32).astype(BF)
            for which in range(2):
                if p != 1:
                    rings[p].buf[block, which, 0] = product[which * size : which * size + size]
                    continue
                ref, n = (v1, k) if k < SPLIT else (w1, k - SPLIT)
                for yi in range(4):
                    at = which * size + yi * 64
                    ref[yi, which, n] = product[at : at + 64]

    def cross_4(which):
        rows = left_4[1, which * 128 : which * 128 + 128]
        for j in range(4):
            right = got[1, :, j * 256 : j * 256 + 256]
            product = lax.dot_general(rows, right, (((1,), (0,)), ((), ())), preferred_element_type=F32).astype(BF)
            for yi in range(4):
                for n in range(2):
                    q4[yi, which, 2 * j + n] = product[yi * 32 : yi * 32 + 32, n * 128 : n * 128 + 128]

    def put_q1(first, count):
        def put(n, side, total):
            k = first + n % count
            ahead = 0
            for i, step in enumerate(ORDER):
                ahead = ahead + step * jnp.where(k == i, 1, 0)
            q1[lax.rem(z + ahead, NZ), n // count, 0] = total.astype(BF)

        return put

    def put_tile_1(which, side, total):
        tile[1, c * (1 - which) + (1 - c) * which] = total

    def put_h4(n, side, total):
        h4[n % 8, n // 8] = total.astype(BF)

    def direct(src, dst, send, recv, size, pos, step_to):
        copies = []
        for d in range(1, size):
            copies.append(
                remote(src.at[lax.rem(pos + d, size)], dst.at[d - 1], send.at[d - 1], recv.at[d - 1], step_to(d))
            )
            copies[-1].start()
        return copies

    def over_y(p):
        def put(which, yi, total):
            if p < 3:
                tile_y[p, yi, which] = total.astype(BF)
            else:
                tile_y[p, yi, which, 0:32] = total.astype(BF)

        rings[p].finish(put, 4)
        rows = slice(0, 64 if p < 3 else 32)
        return direct(tile_y.at[p, :, :, rows], tile_y_r.at[p, :, :, rows], ty_s.at[p], ty_t.at[p], NY, y, on_y)

    def over_x(p, copies):
        for copy in copies:
            copy.wait_recv()
        rows = slice(0, 64 if p < 3 else 32)
        for which in range(2 if p != 1 else 0):
            total = tile_y[p, y, which, rows].astype(F32)
            for d in range(NY - 1):
                total = total + tile_y_r[p, d, which, rows].astype(F32)
            tile[p, c if which == 0 else 1 - c, rows] = total
        if p == 3:
            received("h4")
            for which in range(2):
                total = h4[z, which].astype(F32)
                for d in range(NZ - 1):
                    total = total + h4_r[d, which].astype(F32)
                tile[p, c if which == 0 else 1 - c, 32:64] = total
        flipped = jnp.concatenate([tile[p, 0], tile[p, 1]], axis=0).T
        for side in range(2):
            for n in range(4):
                at = (n % 2) * 32 + side * 16
                mix[p, 2 + side, n] = tile[p, n // 2, at : at + 16, :]
                at = n * 32 + side * 16
                mix[p, side, n] = flipped[at : at + 16]
        out = []
        for d in (1, 2, 3):
            sems = mix_s.at[p, d - 1], mix_t.at[p, d - 1]
            out.append(remote(mix.at[p, lax.rem(x + d, 4)], mix_r.at[p, d - 1], *sems, on_x(d)))
            out[-1].start()
        return out

    def collect(p, copies):
        for copy in copies:
            copy.wait_recv()
        for n in range(4):
            total = -0.5 * ((mix[p, x, n] + mix_r[p, 0, n]) + (mix_r[p, 1, n] + mix_r[p, 2, n]))

            @pl.when(h == 1)
            def _(total=total, n=n):
                summed[2 * p + n % 2, n // 2] = total

            @pl.when(h == 0)
            def _(total=total, n=n):
                at = (p % 2) * 64
                for b in range(2):
                    summed[n * 2 + b, p // 2, :, at : at + 64] = total[:, b * 64 : b * 64 + 64]

    ring_of = {
        "A": ring_a, "B": ring_b, "C": ring_c, "E": ring_e, "Q": ring_4, "V1": ring_v, "W1": ring_w,
        "R0": rings[0], "R1": rings[1], "R2": rings[2], "R3": rings[3],
    }
    sent = {}
    task = {}
    near = dev(2 * h + (1 - l), y, z, c)
    mine = z * h + (y * 2 + c) * (1 - h)

    def do(f):
        task[f.__name__.rstrip("_")] = f
        return f

    def received(name):
        for copy in sent[name]:
            copy.wait_recv()

    def start(name, *copies):
        sent[name] = copies
        for copy in copies:
            copy.start()

    @do
    def gC():
        diag[...] = jnp.zeros_like(diag)
        gram_tiles(x_ref, x_ref, 0, put_c)

    @do
    def gA():
        gram_tiles(x_ref, x_ref, 1, put_a)

    @do
    def gB0():
        mate_copy.wait_recv()
        gram_tiles(mate_x, x_ref, 0, lambda i, tile_: put_y(db, slice(0, 512), i, tile_))

    @do
    def gB1():
        gram_tiles(mate_x, x_ref, 1, lambda i, tile_: put_y(db, slice(512, 1024), i, tile_))

    @do
    def dgy():
        start("dgy", *[remote(diag, diag_y.at[d - 1], dgy_s.at[d - 1], dgy_t.at[d - 1], on_y(d)) for d in range(1, NY)])

    @do
    def dgz():
        received("dgy")
        diag_sum[...] = (diag[...] + diag_y[0]) + (diag_y[1] + diag_y[2])
        start(
            "dgz",
            *[remote(diag_sum, diag_z.at[d - 1], dgz_s.at[d - 1], dgz_t.at[d - 1], on_z(d)) for d in range(1, NZ)],
        )

    @do
    def fcs():
        sent["fc"] = direct(fc, fc_r, fc_s, fc_t, NY, y, on_y)

    @do
    def Ex():
        start("Ex", remote(e_own.at[1 - l], e_near, near_s.at[0], near_t.at[0], near))

    @do
    def Ea():
        received("Ex")

        def add_near(t, _):
            n, half = t // 2, t % 2
            total = e_own[l, n, half].astype(F32) + e_near[n, half].astype(F32)
            e[n, half, 0] = total.astype(BF)
            return _

        lax.fori_loop(0, 16, add_near, 0)

    @do
    def G():
        received("fc")
        total = fc[y].astype(F32)
        for d in range(NY - 1):
            total = total + fc_r[d].astype(F32)
        gc[0] = total[0:16]
        gc[1] = total[16:32]
        received("dgz")
        total = diag_sum[...]
        for d in range(NZ - 1):
            total = total + diag_z[d]
        diag_x[0] = total
        start(
            "G",
            remote(gc.at[1 - l], gc_r, near_s.at[1], near_t.at[1], near),
            remote(diag_x.at[0], diag_x.at[1], near_s.at[2], near_t.at[2], near),
        )

    @do
    def Ef():
        received("G")
        ring_e.finish(put_e)
        row = lax.broadcasted_iota(jnp.int32, (16, W), 0) + (z * 128 + y * 32 + l * 16)
        on_diagonal = lax.broadcasted_iota(jnp.int32, (16, W), 1) == row
        total = jnp.concatenate([gc[l] + gc_r[...], e_sum[0, :, 0:512]], axis=1)
        out_ref[2 * h + c] = -0.5 * (total + jnp.where(on_diagonal, diag_x[0] + diag_x[1], 0.0))
        out_ref[2 * h + 1 - c] = -0.5 * jnp.concatenate([e_sum[0, :, 512:768], e_sum[1]], axis=1)

    @do
    def pieces_():
        def piece_copy(d):
            n = lax.rem(mine + d, 8)
            target = dev(x, y * h + (n // 2) * (1 - h), n * h + z * (1 - h), c * h + (n % 2) * (1 - h))
            return remote(summed.at[n], pieces.at[mine], piece_s.at[d - 1], piece_t.at[d - 1], target)

        start("pieces", *[piece_copy(d) for d in range(1, 8)])
        pieces[mine] = summed[mine]

    @do
    def out():
        received("pieces")

        @pl.when(h == 1)
        def _():
            for s in range(2):
                for n in range(8):
                    out_ref[s, :, n * 128 : n * 128 + 128] = pieces[n, s]

        @pl.when(h == 0)
        def _():
            for s in range(2):
                for n in range(8):
                    at = (n % 4) * 32
                    parts = [pieces[v * 2 + s, n // 4][:, at : at + 32] for v in range(4)]
                    out_ref[2 + s, :, n * 128 : n * 128 + 128] = jnp.concatenate(parts, axis=1)

    task["Af"] = lambda: ring_a.finish(put_ea, 2)
    task["Bf"] = lambda: ring_b.finish(put_eb, 2)
    task["Cf"] = lambda: ring_c.finish(put_fc)
    task["V1f"] = lambda: ring_v.finish(put_q1(0, SPLIT))
    task["W1f"] = lambda: ring_w.finish(put_q1(SPLIT, NZ - SPLIT))
    task["Y1"] = lambda: rings[1].finish(put_tile_1)

    for name, ring in ring_of.items():
        for i in range(ring.size - 1):
            task[f"{name}.{i}"] = functools.partial(ring.step, i)

    def part_tasks(p):
        def send():
            x_wait(0, *range(FROM[p] // 128, FROM[p + 1] // 128))
            start(f"mp{p}", mate_part(p))

        def turn_mate():
            received(f"mp{p}")
            turn(p, 1)

        def cross_group(ks):
            x_wait(1, *ks)
            cross(p, *ks)

        def sum_y():
            sent[f"Y{p}"] = over_y(p)

        def sum_x():
            sent[f"X{p}"] = over_x(p, sent[f"Y{p}"] if p != 1 else ())

        task[f"sp{p}"] = send
        task[f"tu{p}.0"] = lambda: turn(p, 0)
        task[f"tu{p}.1"] = turn_mate
        if p == 4:
            return
        for d, ks in enumerate(GROUPS):
            task[f"cr{p}.{d}"] = functools.partial(cross_group, ks)
        if p != 1:
            task[f"Y{p}"] = sum_y
        task[f"X{p}"] = sum_x
        task[f"K{p}"] = lambda: collect(p, sent[f"X{p}"])
        if p == 1:
            task["ca1"] = lambda: cross_group(tuple(range(SPLIT)))
            task["cb1"] = lambda: cross_group(tuple(range(SPLIT, NZ)))

    for p in range(5):
        part_tasks(p)

    def last_part(which):
        x_wait(1, *range(NZ))
        cross_4(which)

    task["c4.0"] = lambda: last_part(0)
    task["c4.1"] = lambda: last_part(1)

    @do
    def Qf():
        ring_4.finish(put_h4)
        sent["h4"] = direct(h4, h4_r, h4_s, h4_t, NZ, z, on_z)

    for name in SCHEDULE:
        task[name]()
    for ring in ring_of.values():
        ring.drain()
    for copy in x_copies + [mate_copy]:
        copy.wait_send()
    for copies in sent.values():
        for copy in copies:
            copy.wait_send()


def shards(half_ints):
    dma = pltpu.SemaphoreType.DMA
    vmem = pltpu.VMEM
    bufs = [(NY, 2, 4, 32, 512), (NY, 2, 4, 32, W), (NZ, 2, 2, 32, 512), (NZ, 2, 1, 16, 768)]
    bufs += [(NZ, 2, 1, 256, 128), (NZ, 2, 1, 64, 128), (NZ, 2, 1, 256, 128), (NZ, 2, 1, 128, 128)]
    bufs += [(NY, 2, 8, 32, 128), (NY, 2, SPLIT, 64, 128), (NY, 2, NZ - SPLIT, 64, 128)]
    scratch = [vmem((3, OCC, W), BF), vmem((K, W), BF), vmem((K, W), BF)]
    scratch += [vmem((2, KH, W), BF), vmem((KH, W), BF), vmem((3, 512, KH), BF), vmem((2, 256, KH), BF)]
    scratch += [vmem(shape, BF) for shape in bufs]
    scratch += [vmem((2, shape[0] - 1) + shape[2:], BF) for shape in bufs]
    scratch += [
        vmem((2, NZ, 2, 16, 768), BF),
        vmem((NZ, 2, 16, 768), BF),
        vmem((2, 16, 768), F32),
        vmem((NY, 32, 512), BF),
        vmem((NY - 1, 32, 512), BF),
        vmem((2, 16, 512), F32),
        vmem((16, 512), F32),
        vmem((NZ, 2, 32, 128), BF),
        vmem((NZ - 1, 2, 32, 128), BF),
        vmem((PARTS, NY, 2, 64, 128), BF),
        vmem((PARTS, NY - 1, 2, 64, 128), BF),
        vmem((PARTS, 2, 64, 128), F32),
        vmem((PARTS, 4, 4, 16, 128), F32),
        vmem((PARTS, 3, 4, 16, 128), F32),
        vmem((8, 2, 16, 128), F32),
        vmem((8, 2, 16, 128), F32),
        vmem((1, W), F32),
        vmem((1, W), F32),
        vmem((NY - 1, 1, W), F32),
        vmem((NZ - 1, 1, W), F32),
        vmem((2, 1, W), F32),
    ]
    for shape in bufs:
        scratch += [dma((2, shape[0] - 1))] * 2
    scratch += [dma((3,))] + [dma((2, NZ))] * 2 + [dma((6,))] * 2 + [dma((3,))] * 2
    scratch += [dma((PARTS, NY - 1))] * 2 + [dma((PARTS, 3))] * 2 + [dma((7,))] * 2
    scratch += [dma((NY - 1,))] * 2 + [dma((NZ - 1,))] * 2 + [dma((NY - 1,))] * 2 + [dma((NZ - 1,))] * 2
    out = pl.pallas_call(
        kernel,
        out_shape=jax.ShapeDtypeStruct((4, 16, W), F32),
        in_specs=[pl.BlockSpec(memory_space=pl.ANY)],
        out_specs=pl.BlockSpec(memory_space=pltpu.VMEM),
        scratch_shapes=scratch,
        compiler_params=pltpu.CompilerParams(
            collective_id=0, has_side_effects=True, vmem_limit_bytes=56 * 1024 * 1024
        ),
        cost_estimate=pl.CostEstimate(flops=2 * 1024 * 1024 * K * 3, bytes_accessed=4 << 20, transcendentals=0),
    )(half_ints)
    return out.transpose(1, 0, 2)


def solution(mesh):
    placed = (P("aux", None, "rows"),)
    return jax.shard_map(
        shards, mesh=mesh, in_specs=placed, out_specs=P("aux", None, "rows"), check_vma=False
    )
```

time: 98 us -> 82.7 us (0.84)
  Pallas kernels: 96.1 us -> 80.8 us
    pallas_call x1, Pallas kernels: 96.1 us -> 80.8 us  [shards(): pl.pallas_call(kernel, out_shape=jax.ShapeDtypeStruct((4, 16, W), F32), i...]
where the time goes in v4:
time: 82.7 us; the launch traced here: 82.6 us
  Pallas kernels  80.8 us (98%)
  local copies, waits for them, and re-layouts  1.82 us (2%)
    pallas_call x1, Pallas kernels, shards(): pl.pallas_call(kernel, out_shape=jax.ShapeDtypeStruct((4, 16, W), F32), i...  80.8 us
    transpose x1, local copies, waits for them, and re-layouts, shards(): return out.transpose(1, 0, 2)  1.82 us

profile of v4, /device:TPU:1, one launch (start us, length us, event | category | flops | bytes accessed | tf_op | source)
XLA Modules:
  0.0 82.6 jit_solution(4361899974058688222)
XLA Ops:
  0.0 80.8 %shard_map.17 = f32[4,16,1024]{2,1,0:T(8,128)} custom-call(bf16[3,500,1024]{2,1,0:T(8,128)(2,1)} %half_ints.1), custom_call_target="tpu_custom_call" | custom-call | flops 9663676416 | bytes 4194304 | tf_op jit(solution)/shard_map/pallas_call | solution.py:618
  80.8 1.8 %copy.2 = f32[16,4,1024]{2,1,0:T(4,128)} copy(f32[16,4,1024]{2,0,1:T(8,128)} %bitcast.1) | data formatting | bytes 524288 | tf_op jit(solution)/shard_map/transpose | solution.py:629

commit v5 on v4

--- a/solution.py
+++ b/solution.py
@@ -16,18 +16,21 @@
 KH = K // 2
 ORDER = (4, 3, 5, 2, 6, 1, 7, 0)
 PARTS = 4
-SPLIT = 5
+SPLITS = (0, 5, 7, 8)
+EARLY = 2
+CZ, CW = 768, 768
+CA, EH = W - CZ, W - CZ // 2
 GROUPS = ((7,), (5, 6), (3, 4), (1, 2), (0,))
 SCHEDULE = (
-    "gC", "gA", "A.0", "A.1", "C.0", "C.1", "gB0", "gB1", "sp0", "A.2", "tu0.0", "C.2", "C.3", "B.0", "B.1", "tu0.1",
-    "cr0.3", "cr0.4", "R0.0", "R0.1", "C.4", "Af", "C.5", "sp1", "tu1.0", "R0.2", "tu1.1", "C.6", "cr0.2", "R0.3",
-    "ca1", "V1.0", "B.2", "V1.1", "R0.4", "Cf", "fcs", "sp2", "tu2.0", "tu2.1", "cr2.4", "R2.0", "cr2.3", "R2.1",
-    "cr2.2", "V1.2", "sp3", "cr0.1", "R0.5", "tu3.0", "cr2.1", "R0.6", "tu3.1", "cr3.1", "cr3.4", "R3.0", "R2.2",
-    "cr3.3", "R3.1", "cr3.2", "R2.3", "cr0.0", "sp4", "cb1", "W1.0", "W1.1", "Bf", "Ex", "tu4.0", "Y0", "tu4.1",
-    "cr2.0", "R3.2", "c4.0", "c4.1", "Q.0", "dgy", "R2.4", "Q.1", "cr3.0", "R3.3", "V1f", "R1.0", "R1.1", "R2.5",
-    "W1.2", "R3.4", "R2.6", "X0", "R1.2", "R3.5", "R1.3", "Q.2", "dgz", "R3.6", "W1f", "Ea", "R1.4", "E.0", "Y2",
-    "Qf", "R1.5", "E.1", "K0", "G", "Y3", "R1.6", "E.2", "X2", "X3", "E.3", "Y1", "X1", "E.4", "K2", "E.5", "K3",
-    "E.6", "K1", "pieces", "Ef", "out",
+    "gC0", "C0.0", "gA", "A.0", "A.1", "C0.1", "gB0", "C0.2", "gB1", "A.2", "sp0", "B.0", "B.1", "tu0.0", "C0.3",
+    "C0.4", "tu0.1", "cr0.3", "cr0.4", "R0.0", "R0.1", "Af", "C0.5", "sp1", "tu1.0", "C0.6", "R0.2", "tu1.1", "cr1.4",
+    "R1.0", "cr1.3", "B.2", "R1.1", "cr0.2", "R0.3", "cr1.2", "Cf", "fcs", "sp2", "tu2.0", "R0.4", "R1.2", "tu2.1",
+    "cV2", "V2.0", "V2.1", "R1.3", "sp3", "cr0.1", "cr1.1", "R0.5", "Bf", "dgy", "cU2", "R0.6", "tu3.0", "U2.0",
+    "U2.1", "tu3.1", "cr3.2", "cr3.1", "cr3.3", "cr3.4", "R3.0", "R3.1", "R1.4", "R1.5", "Ex", "cr1.0", "cW2", "V2.2",
+    "cr3.0", "W2.0", "W2.1", "sp4", "cr0.0", "tu4.0", "c4.0", "dgz", "Y0", "tu4.1", "c4.1", "Q.0", "U2.2", "R3.2",
+    "Q.1", "R3.3", "V2f", "R2.0", "R1.6", "R2.1", "W2.2", "X0", "G", "R3.4", "Q.2", "R3.5", "R2.2", "Ea", "U2f",
+    "E.0", "E.1", "Y1", "R2.3", "W2f", "K0", "R3.6", "R2.4", "Qf", "E.2", "E.3", "R2.5", "X1", "Y3", "R2.6", "X3",
+    "K1", "E.4", "pieces0", "E.5", "Y2", "X2", "E.6", "K3", "K2", "pieces1", "Ef", "out",
 )
 FROM = (0, 256, 512, 768, 896, 1024)
 OCC = 500
@@ -106,10 +109,10 @@
                 self.copy(direction, i).wait_send()
 
 
-def gram_tiles(lhs, rhs, j, put):
+def gram_tiles(lhs, rhs, first, width, put):
     def body(i, _):
         left = lhs[:, pl.ds(pl.multiple_of(i * 256, 256), 256)]
-        right = rhs[:, j * 512 : j * 512 + 512]
+        right = rhs[:, first : first + width]
         tile = lax.dot_general(left, right, (((0,), (0,)), ((), ())), preferred_element_type=F32)
         put(i, tile)
         return _
@@ -119,12 +122,13 @@
 
 def kernel(
     half_ints, out_ref, raw, x_ref, mate_x, got, mate_got, left, left_4,
-    da, db, dc, e, q0, q1, q2, q3, q4, v1, w1,
-    da_r, db_r, dc_r, e_r, q0_r, q1_r, q2_r, q3_r, q4_r, v1_r, w1_r,
+    da, db, dc0, e, q0, q1, q2, q3, q4, v2, u2, w2,
+    da_r, db_r, dc0_r, e_r, q0_r, q1_r, q2_r, q3_r, q4_r, v2_r, u2_r, w2_r,
     e_own, e_near, e_sum, fc, fc_r, gc, gc_r, h4, h4_r,
     tile_y, tile_y_r, tile, mix, mix_r, summed, pieces, diag, diag_sum, diag_y, diag_z, diag_x,
-    da_s, da_t, db_s, db_t, dc_s, dc_t, e_s, e_t, q0_s, q0_t, q1_s, q1_t, q2_s, q2_t, q3_s, q3_t, q4_s, q4_t, v1_s, v1_t, w1_s, w1_t,
-    raw_t, x_s, x_t, mate_s, mate_t, near_s, near_t, ty_s, ty_t, mix_s, mix_t, piece_s, piece_t,
+    da_s, da_t, db_s, db_t, dc0_s, dc0_t, e_s, e_t,
+    q0_s, q0_t, q1_s, q1_t, q2_s, q2_t, q3_s, q3_t, q4_s, q4_t, v2_s, v2_t, u2_s, u2_t, w2_s, w2_t,
+    raw_t, x_s, x_t, mate_s, mate_t, near_s, near_t, ty_s, ty_t, mix_s, mix_t, piece_s, piece_t, piece0_s, piece0_t,
     dgy_s, dgy_t, dgz_s, dgz_t, fc_s, fc_t, h4_s, h4_t,
 ):
     raw_copies = [pltpu.make_async_copy(half_ints.at[p], raw.at[p], raw_t.at[p]) for p in range(3)]
@@ -207,7 +211,9 @@
 
     ring_a = y_ring(da, da_r, da_s, da_t)
     ring_b = y_ring(db, db_r, db_s, db_t)
-    ring_c = z_ring(dc, dc_r, dc_s, dc_t)
+    rings_c = [
+        z_ring(dc0, dc0_r, dc0_s, dc0_t),
+    ]
     ring_e = z_ring(e, e_r, e_s, e_t)
     rings = [
         z_ring(q0, q0_r, q0_s, q0_t),
@@ -216,13 +222,12 @@
         z_ring(q3, q3_r, q3_s, q3_t),
     ]
     ring_4 = y_ring(q4, q4_r, q4_s, q4_t)
-    ring_v = y_ring(v1, v1_r, v1_s, v1_t)
-    ring_w = y_ring(w1, w1_r, w1_s, w1_t)
-
-    def no_diagonal(i, j, tile_):
-        on_diagonal = lax.broadcasted_iota(jnp.int32, (256, 512), 1) - lax.broadcasted_iota(jnp.int32, (256, 512), 0)
-        on_diagonal = on_diagonal == i * 256 - j * 512
-        diag[:, j * 512 : j * 512 + 512] += jnp.sum(jnp.where(on_diagonal, tile_, 0.0), axis=0, keepdims=True)
+    rings_early = [y_ring(v2, v2_r, v2_s, v2_t), y_ring(u2, u2_r, u2_s, u2_t), y_ring(w2, w2_r, w2_s, w2_t)]
+
+    def no_diagonal(i, first, tile_):
+        ahead = lax.broadcasted_iota(jnp.int32, tile_.shape, 1) - lax.broadcasted_iota(jnp.int32, tile_.shape, 0)
+        on_diagonal = ahead == i * 256 - first
+        diag[:, first : first + tile_.shape[1]] += jnp.sum(jnp.where(on_diagonal, tile_, 0.0), axis=0, keepdims=True)
         return jnp.where(on_diagonal, 0.0, tile_)
 
     def put_y(ref, columns, i, tile_):
@@ -234,23 +239,29 @@
                 ref[yi, zi // 4, zi % 4, :, columns] = rows
 
     def put_a(i, tile_):
-        put_y(da, slice(0, 512), i, no_diagonal(i, 1, tile_))
-
-    def put_c(i, tile_):
-        tile_ = no_diagonal(i, 0, tile_).astype(BF)
-        for k in range(2):
-            for yi in range(4):
-                dc[2 * i + k, yi // 2, yi % 2] = tile_[k * 128 + yi * 32 : k * 128 + yi * 32 + 32]
+        put_y(da, slice(0, CA), i, no_diagonal(i, CZ, tile_))
+
+    def put_c(n):
+        def put(i, tile_):
+            tile_ = no_diagonal(i, n * CW, tile_).astype(BF)
+            for k in range(2):
+                for yi in range(4):
+                    rings_c[n].buf[2 * i + k, yi // 2, yi % 2] = tile_[k * 128 + yi * 32 : k * 128 + yi * 32 + 32]
+
+        return put
 
     def put_ea(n, side, total):
-        e_own[side, n, 0, :, 0:512] = total.astype(BF)
+        e_own[side, n, 0, :, 0:CA] = total.astype(BF)
 
     def put_eb(n, side, total):
-        e_own[side, n, 0, :, 512:768] = total[:, 0:256].astype(BF)
-        e_own[side, n, 1] = total[:, 256:1024].astype(BF)
-
-    def put_fc(n, side, total):
-        fc[n] = total.astype(BF)
+        e_own[side, n, 0, :, CA:EH] = total[:, 0 : EH - CA].astype(BF)
+        e_own[side, n, 1] = total[:, EH - CA : W].astype(BF)
+
+    def put_fc(k):
+        def put(n, side, total):
+            fc[n, :, k * CW : k * CW + CW] = total.astype(BF)
+
+        return put
 
     def put_e(half, part, total):
         e_sum[half] = total
@@ -277,13 +288,13 @@
             rows = left[p] if p < 3 else left_4[p - 3]
             product = lax.dot_general(rows, right, (((1,), (0,)), ((), ())), preferred_element_type=F32).astype(BF)
             for which in range(2):
-                if p != 1:
+                if p != EARLY:
                     rings[p].buf[block, which, 0] = product[which * size : which * size + size]
                     continue
-                ref, n = (v1, k) if k < SPLIT else (w1, k - SPLIT)
+                i = max(i for i in range(3) if SPLITS[i] <= k)
                 for yi in range(4):
                     at = which * size + yi * 64
-                    ref[yi, which, n] = product[at : at + 64]
+                    rings_early[i].buf[yi, which, k - SPLITS[i]] = product[at : at + 64]
 
     def cross_4(which):
         rows = left_4[1, which * 128 : which * 128 + 128]
@@ -294,18 +305,18 @@
                 for n in range(2):
                     q4[yi, which, 2 * j + n] = product[yi * 32 : yi * 32 + 32, n * 128 : n * 128 + 128]
 
-    def put_q1(first, count):
+    def put_early(first, count):
         def put(n, side, total):
             k = first + n % count
             ahead = 0
             for i, step in enumerate(ORDER):
                 ahead = ahead + step * jnp.where(k == i, 1, 0)
-            q1[lax.rem(z + ahead, NZ), n // count, 0] = total.astype(BF)
+            rings[EARLY].buf[lax.rem(z + ahead, NZ), n // count, 0] = total.astype(BF)
 
         return put
 
-    def put_tile_1(which, side, total):
-        tile[1, c * (1 - which) + (1 - c) * which] = total
+    def put_tile_early(which, side, total):
+        tile[EARLY, c * (1 - which) + (1 - c) * which] = total
 
     def put_h4(n, side, total):
         h4[n % 8, n // 8] = total.astype(BF)
@@ -334,7 +345,7 @@
         for copy in copies:
             copy.wait_recv()
         rows = slice(0, 64 if p < 3 else 32)
-        for which in range(2 if p != 1 else 0):
+        for which in range(2 if p != EARLY else 0):
             total = tile_y[p, y, which, rows].astype(F32)
             for d in range(NY - 1):
                 total = total + tile_y_r[p, d, which, rows].astype(F32)
@@ -368,22 +379,22 @@
 
             @pl.when(h == 1)
             def _(total=total, n=n):
-                summed[2 * p + n % 2, n // 2] = total
+                summed[p // 2, 4 * (p % 2) + n % 2 * 2 + n // 2] = total
 
             @pl.when(h == 0)
             def _(total=total, n=n):
                 at = (p % 2) * 64
                 for b in range(2):
-                    summed[n * 2 + b, p // 2, :, at : at + 64] = total[:, b * 64 : b * 64 + 64]
-
-    ring_of = {
-        "A": ring_a, "B": ring_b, "C": ring_c, "E": ring_e, "Q": ring_4, "V1": ring_v, "W1": ring_w,
-        "R0": rings[0], "R1": rings[1], "R2": rings[2], "R3": rings[3],
-    }
+                    summed[p // 2, n * 2 + b, :, at : at + 64] = total[:, b * 64 : b * 64 + 64]
+
+    ring_of = {"A": ring_a, "B": ring_b, "E": ring_e, "Q": ring_4}
+    ring_of.update({f"C{i}": ring for i, ring in enumerate(rings_c)})
+    ring_of.update({f"R{i}": ring for i, ring in enumerate(rings)})
+    ring_of.update({f"{i}{EARLY}": ring for i, ring in zip("VUW", rings_early)})
     sent = {}
     task = {}
     near = dev(2 * h + (1 - l), y, z, c)
-    mine = z * h + (y * 2 + c) * (1 - h)
+    mine = y * 2 + c
 
     def do(f):
         task[f.__name__.rstrip("_")] = f
@@ -398,23 +409,26 @@
         for copy in copies:
             copy.start()
 
-    @do
-    def gC():
-        diag[...] = jnp.zeros_like(diag)
-        gram_tiles(x_ref, x_ref, 0, put_c)
+    def gC(n):
+        if n == 0:
+            diag[...] = jnp.zeros_like(diag)
+        gram_tiles(x_ref, x_ref, n * CW, CW, put_c(n))
+
+    for n in range(CZ // CW):
+        task[f"gC{n}"] = functools.partial(gC, n)
 
     @do
     def gA():
-        gram_tiles(x_ref, x_ref, 1, put_a)
+        gram_tiles(x_ref, x_ref, CZ, CA, put_a)
 
     @do
     def gB0():
         mate_copy.wait_recv()
-        gram_tiles(mate_x, x_ref, 0, lambda i, tile_: put_y(db, slice(0, 512), i, tile_))
+        gram_tiles(mate_x, x_ref, 0, 512, lambda i, tile_: put_y(db, slice(0, 512), i, tile_))
 
     @do
     def gB1():
-        gram_tiles(mate_x, x_ref, 1, lambda i, tile_: put_y(db, slice(512, 1024), i, tile_))
+        gram_tiles(mate_x, x_ref, 512, 512, lambda i, tile_: put_y(db, slice(512, 1024), i, tile_))
 
     @do
     def dgy():
@@ -474,32 +488,64 @@
         ring_e.finish(put_e)
         row = lax.broadcasted_iota(jnp.int32, (16, W), 0) + (z * 128 + y * 32 + l * 16)
         on_diagonal = lax.broadcasted_iota(jnp.int32, (16, W), 1) == row
-        total = jnp.concatenate([gc[l] + gc_r[...], e_sum[0, :, 0:512]], axis=1)
+        total = jnp.concatenate([gc[l] + gc_r[...], e_sum[0, :, 0:CA]], axis=1)
         out_ref[2 * h + c] = -0.5 * (total + jnp.where(on_diagonal, diag_x[0] + diag_x[1], 0.0))
-        out_ref[2 * h + 1 - c] = -0.5 * jnp.concatenate([e_sum[0, :, 512:768], e_sum[1]], axis=1)
-
-    @do
-    def pieces_():
-        def piece_copy(d):
-            n = lax.rem(mine + d, 8)
-            target = dev(x, y * h + (n // 2) * (1 - h), n * h + z * (1 - h), c * h + (n % 2) * (1 - h))
-            return remote(summed.at[n], pieces.at[mine], piece_s.at[d - 1], piece_t.at[d - 1], target)
-
-        start("pieces", *[piece_copy(d) for d in range(1, 8)])
-        pieces[mine] = summed[mine]
-
-    @do
-    def out():
-        received("pieces")
-
+        out_ref[2 * h + 1 - c] = -0.5 * jnp.concatenate([e_sum[0, :, CA:EH], e_sum[1]], axis=1)
+
+    def row_piece(n):
+        src = summed.at[n // 4, n % 4 * 2 : n % 4 * 2 + 2]
+        return remote(src, pieces.at[z], piece_s.at[n], piece_t.at[z], dev(x, y, n, c))
+
+    def row_wait(n):
+        src = summed.at[n // 4, n % 4 * 2 : n % 4 * 2 + 2]
+        return remote(src, pieces.at[n], piece_s.at[n], piece_t.at[n], dev(x, y, n, c))
+
+    def column_piece(q, d):
+        n = lax.rem(mine + d, 8)
+        sems = piece0_s.at[q, d - 1], piece0_t.at[q, d - 1]
+        return remote(summed.at[q, n], pieces.at[mine, q], *sems, dev(x, n // 2, z, n % 2))
+
+    def send_pieces(q):
         @pl.when(h == 1)
         def _():
+            for n in range(4 * q, 4 * q + 4):
+
+                @pl.when(n != z)
+                def _(n=n):
+                    row_piece(n).start()
+
+                @pl.when(n == z)
+                def _(n=n):
+                    pieces[n] = summed[q, n % 4 * 2 : n % 4 * 2 + 2]
+
+        @pl.when(h == 0)
+        def _():
+            for d in range(1, 8):
+                column_piece(q, d).start()
+            pieces[mine, q] = summed[q, mine]
+
+    task["pieces0"] = lambda: send_pieces(0)
+    task["pieces1"] = lambda: send_pieces(1)
+
+    @do
+    def out():
+        @pl.when(h == 1)
+        def _():
+            for n in range(8):
+
+                @pl.when(n != z)
+                def _(n=n):
+                    row_wait(n).wait()
+
             for s in range(2):
                 for n in range(8):
                     out_ref[s, :, n * 128 : n * 128 + 128] = pieces[n, s]
 
         @pl.when(h == 0)
         def _():
+            for q in range(2):
+                for d in range(1, 8):
+                    column_piece(q, d).wait()
             for s in range(2):
                 for n in range(8):
                     at = (n % 4) * 32
@@ -508,10 +554,16 @@
 
     task["Af"] = lambda: ring_a.finish(put_ea, 2)
     task["Bf"] = lambda: ring_b.finish(put_eb, 2)
-    task["Cf"] = lambda: ring_c.finish(put_fc)
-    task["V1f"] = lambda: ring_v.finish(put_q1(0, SPLIT))
-    task["W1f"] = lambda: ring_w.finish(put_q1(SPLIT, NZ - SPLIT))
-    task["Y1"] = lambda: rings[1].finish(put_tile_1)
+    for n, letter in enumerate("VUW"):
+        count = SPLITS[n + 1] - SPLITS[n]
+        task[f"{letter}{EARLY}f"] = functools.partial(rings_early[n].finish, put_early(SPLITS[n], count))
+    task[f"Y{EARLY}"] = lambda: rings[EARLY].finish(put_tile_early)
+
+    @do
+    def Cf():
+        for n, ring in enumerate(rings_c):
+            ring.finish(put_fc(n))
+
 
     for name, ring in ring_of.items():
         for i in range(ring.size - 1):
@@ -534,7 +586,7 @@
             sent[f"Y{p}"] = over_y(p)
 
         def sum_x():
-            sent[f"X{p}"] = over_x(p, sent[f"Y{p}"] if p != 1 else ())
+            sent[f"X{p}"] = over_x(p, sent[f"Y{p}"] if p != EARLY else ())
 
         task[f"sp{p}"] = send
         task[f"tu{p}.0"] = lambda: turn(p, 0)
@@ -543,13 +595,13 @@
             return
         for d, ks in enumerate(GROUPS):
             task[f"cr{p}.{d}"] = functools.partial(cross_group, ks)
-        if p != 1:
+        if p != EARLY:
             task[f"Y{p}"] = sum_y
         task[f"X{p}"] = sum_x
         task[f"K{p}"] = lambda: collect(p, sent[f"X{p}"])
-        if p == 1:
-            task["ca1"] = lambda: cross_group(tuple(range(SPLIT)))
-            task["cb1"] = lambda: cross_group(tuple(range(SPLIT, NZ)))
+        if p == EARLY:
+            for n, letter in enumerate("VUW"):
+                task[f"c{letter}{EARLY}"] = functools.partial(cross_group, tuple(range(SPLITS[n], SPLITS[n + 1])))
 
     for p in range(5):
         part_tasks(p)
@@ -580,21 +632,22 @@
 def shards(half_ints):
     dma = pltpu.SemaphoreType.DMA
     vmem = pltpu.VMEM
-    bufs = [(NY, 2, 4, 32, 512), (NY, 2, 4, 32, W), (NZ, 2, 2, 32, 512), (NZ, 2, 1, 16, 768)]
-    bufs += [(NZ, 2, 1, 256, 128), (NZ, 2, 1, 64, 128), (NZ, 2, 1, 256, 128), (NZ, 2, 1, 128, 128)]
-    bufs += [(NY, 2, 8, 32, 128), (NY, 2, SPLIT, 64, 128), (NY, 2, NZ - SPLIT, 64, 128)]
+    bufs = [(NY, 2, 4, 32, CA), (NY, 2, 4, 32, W)] + [(NZ, 2, 2, 32, CW)] * (CZ // CW) + [(NZ, 2, 1, 16, EH)]
+    bufs += [(NZ, 2, 1, 64 if p == EARLY else 256, 128) for p in range(3)]
+    bufs += [(NZ, 2, 1, 128, 128), (NY, 2, 8, 32, 128)]
+    bufs += [(NY, 2, SPLITS[i + 1] - SPLITS[i], 64, 128) for i in range(3)]
     scratch = [vmem((3, OCC, W), BF), vmem((K, W), BF), vmem((K, W), BF)]
     scratch += [vmem((2, KH, W), BF), vmem((KH, W), BF), vmem((3, 512, KH), BF), vmem((2, 256, KH), BF)]
     scratch += [vmem(shape, BF) for shape in bufs]
     scratch += [vmem((2, shape[0] - 1) + shape[2:], BF) for shape in bufs]
     scratch += [
-        vmem((2, NZ, 2, 16, 768), BF),
-        vmem((NZ, 2, 16, 768), BF),
-        vmem((2, 16, 768), F32),
-        vmem((NY, 32, 512), BF),
-        vmem((NY - 1, 32, 512), BF),
-        vmem((2, 16, 512), F32),
-        vmem((16, 512), F32),
+        vmem((2, NZ, 2, 16, EH), BF),
+        vmem((NZ, 2, 16, EH), BF),
+        vmem((2, 16, EH), F32),
+        vmem((NY, 32, CZ), BF),
+        vmem((NY - 1, 32, CZ), BF),
+        vmem((2, 16, CZ), F32),
+        vmem((16, CZ), F32),
         vmem((NZ, 2, 32, 128), BF),
         vmem((NZ - 1, 2, 32, 128), BF),
         vmem((PARTS, NY, 2, 64, 128), BF),
@@ -602,7 +655,7 @@
         vmem((PARTS, 2, 64, 128), F32),
         vmem((PARTS, 4, 4, 16, 128), F32),
         vmem((PARTS, 3, 4, 16, 128), F32),
-        vmem((8, 2, 16, 128), F32),
+        vmem((2, 8, 16, 128), F32),
         vmem((8, 2, 16, 128), F32),
         vmem((1, W), F32),
         vmem((1, W), F32),
@@ -613,7 +666,7 @@
     for shape in bufs:
         scratch += [dma((2, shape[0] - 1))] * 2
     scratch += [dma((3,))] + [dma((2, NZ))] * 2 + [dma((6,))] * 2 + [dma((3,))] * 2
-    scratch += [dma((PARTS, NY - 1))] * 2 + [dma((PARTS, 3))] * 2 + [dma((7,))] * 2
+    scratch += [dma((PARTS, NY - 1))] * 2 + [dma((PARTS, 3))] * 2 + [dma((NZ,))] * 2 + [dma((2, 7))] * 2
     scratch += [dma((NY - 1,))] * 2 + [dma((NZ - 1,))] * 2 + [dma((NY - 1,))] * 2 + [dma((NZ - 1,))] * 2
     out = pl.pallas_call(
         kernel,

time: 82.7 us -> 81.9 us (level)
  Pallas kernels: 80.8 us -> 79.9 us
    pallas_call x1, Pallas kernels: 80.8 us -> 79.9 us  [shards(): pl.pallas_call(kernel, out_shape=jax.ShapeDtypeStruct((4, 16, W), F32), i...]
where the time goes in v5:
time: 81.9 us; the launch traced here: 81.7 us
  Pallas kernels  79.9 us (98%)
  local copies, waits for them, and re-layouts  1.82 us (2%)
    pallas_call x1, Pallas kernels, shards(): pl.pallas_call(kernel, out_shape=jax.ShapeDtypeStruct((4, 16, W), F32), i...  79.9 us
    transpose x1, local copies, waits for them, and re-layouts, shards(): return out.transpose(1, 0, 2)  1.82 us

profile of v5, /device:TPU:1, one launch (start us, length us, event | category | flops | bytes accessed | tf_op | source)
XLA Modules:
  0.0 81.7 jit_solution(14610151106618364292)
XLA Ops:
  0.0 79.9 %shard_map.17 = f32[4,16,1024]{2,1,0:T(8,128)} custom-call(bf16[3,500,1024]{2,1,0:T(8,128)(2,1)} %half_ints.1), custom_call_target="tpu_custom_call" | custom-call | flops 9663676416 | bytes 4194304 | tf_op jit(solution)/shard_map/pallas_call | solution.py:671
  79.9 1.8 %copy.2 = f32[16,4,1024]{2,1,0:T(4,128)} copy(f32[16,4,1024]{2,0,1:T(8,128)} %bitcast.1) | data formatting | bytes 524288 | tf_op jit(solution)/shard_map/transpose | solution.py:682

commit v6 on v5

--- a/solution.py
+++ b/solution.py
@@ -30,7 +30,7 @@
     "cr3.0", "W2.0", "W2.1", "sp4", "cr0.0", "tu4.0", "c4.0", "dgz", "Y0", "tu4.1", "c4.1", "Q.0", "U2.2", "R3.2",
     "Q.1", "R3.3", "V2f", "R2.0", "R1.6", "R2.1", "W2.2", "X0", "G", "R3.4", "Q.2", "R3.5", "R2.2", "Ea", "U2f",
     "E.0", "E.1", "Y1", "R2.3", "W2f", "K0", "R3.6", "R2.4", "Qf", "E.2", "E.3", "R2.5", "X1", "Y3", "R2.6", "X3",
-    "K1", "E.4", "pieces0", "E.5", "Y2", "X2", "E.6", "K3", "K2", "pieces1", "Ef", "out",
+    "K1", "E.4", "pieces0", "E.5", "Y2", "X2", "E.6", "K3", "K2", "pieces1", "Ef",
 )
 FROM = (0, 256, 512, 768, 896, 1024)
 OCC = 500
@@ -125,7 +125,7 @@
     da, db, dc0, e, q0, q1, q2, q3, q4, v2, u2, w2,
     da_r, db_r, dc0_r, e_r, q0_r, q1_r, q2_r, q3_r, q4_r, v2_r, u2_r, w2_r,
     e_own, e_near, e_sum, fc, fc_r, gc, gc_r, h4, h4_r,
-    tile_y, tile_y_r, tile, mix, mix_r, summed, pieces, diag, diag_sum, diag_y, diag_z, diag_x,
+    tile_y, tile_y_r, tile, mix, mix_b, mix_r, summed, pieces, diag, diag_sum, diag_y, diag_z, diag_x,
     da_s, da_t, db_s, db_t, dc0_s, dc0_t, e_s, e_t,
     q0_s, q0_t, q1_s, q1_t, q2_s, q2_t, q3_s, q3_t, q4_s, q4_t, v2_s, v2_t, u2_s, u2_t, w2_s, w2_t,
     raw_t, x_s, x_t, mate_s, mate_t, near_s, near_t, ty_s, ty_t, mix_s, mix_t, piece_s, piece_t, piece0_s, piece0_t,
@@ -364,10 +364,11 @@
                 mix[p, 2 + side, n] = tile[p, n // 2, at : at + 16, :]
                 at = n * 32 + side * 16
                 mix[p, side, n] = flipped[at : at + 16]
+        mix_b[p] = mix[p].astype(BF)
         out = []
         for d in (1, 2, 3):
             sems = mix_s.at[p, d - 1], mix_t.at[p, d - 1]
-            out.append(remote(mix.at[p, lax.rem(x + d, 4)], mix_r.at[p, d - 1], *sems, on_x(d)))
+            out.append(remote(mix_b.at[p, lax.rem(x + d, 4)], mix_r.at[p, d - 1], *sems, on_x(d)))
             out[-1].start()
         return out
 
@@ -375,7 +376,8 @@
         for copy in copies:
             copy.wait_recv()
         for n in range(4):
-            total = -0.5 * ((mix[p, x, n] + mix_r[p, 0, n]) + (mix_r[p, 1, n] + mix_r[p, 2, n]))
+            total = mix[p, x, n] + mix_r[p, 0, n].astype(F32)
+            total = -0.5 * (total + (mix_r[p, 1, n].astype(F32) + mix_r[p, 2, n].astype(F32)))
 
             @pl.when(h == 1)
             def _(total=total, n=n):
@@ -546,11 +548,11 @@
             for q in range(2):
                 for d in range(1, 8):
                     column_piece(q, d).wait()
-            for s in range(2):
-                for n in range(8):
-                    at = (n % 4) * 32
-                    parts = [pieces[v * 2 + s, n // 4][:, at : at + 32] for v in range(4)]
-                    out_ref[2 + s, :, n * 128 : n * 128 + 128] = jnp.concatenate(parts, axis=1)
+                for s in range(2):
+                    for n in range(4):
+                        parts = [pieces[v * 2 + s, q][:, n * 32 : n * 32 + 32] for v in range(4)]
+                        at = q * 512 + n * 128
+                        out_ref[2 + s, :, at : at + 128] = jnp.concatenate(parts, axis=1)
 
     task["Af"] = lambda: ring_a.finish(put_ea, 2)
     task["Bf"] = lambda: ring_b.finish(put_eb, 2)
@@ -627,6 +629,7 @@
     for copies in sent.values():
         for copy in copies:
             copy.wait_send()
+    out()
 
 
 def shards(half_ints):
@@ -654,7 +657,8 @@
         vmem((PARTS, NY - 1, 2, 64, 128), BF),
         vmem((PARTS, 2, 64, 128), F32),
         vmem((PARTS, 4, 4, 16, 128), F32),
-        vmem((PARTS, 3, 4, 16, 128), F32),
+        vmem((PARTS, 4, 4, 16, 128), BF),
+        vmem((PARTS, 3, 4, 16, 128), BF),
         vmem((2, 8, 16, 128), F32),
         vmem((8, 2, 16, 128), F32),
         vmem((1, W), F32),

time: 81.9 us -> 80.7 us (0.985)
  Pallas kernels: 79.9 us -> 78.8 us
    pallas_call x1, Pallas kernels: 79.9 us -> 78.8 us  [shards(): pl.pallas_call(kernel, out_shape=jax.ShapeDtypeStruct((4, 16, W), F32), i...]
where the time goes in v6:
time: 80.7 us; the launch traced here: 80.6 us
  Pallas kernels  78.8 us (98%)
  local copies, waits for them, and re-layouts  1.82 us (2%)
    pallas_call x1, Pallas kernels, shards(): pl.pallas_call(kernel, out_shape=jax.ShapeDtypeStruct((4, 16, W), F32), i...  78.8 us
    transpose x1, local copies, waits for them, and re-layouts, shards(): return out.transpose(1, 0, 2)  1.82 us

profile of v6, /device:TPU:1, one launch (start us, length us, event | category | flops | bytes accessed | tf_op | source)
XLA Modules:
  0.0 80.6 jit_solution(3512275682362959853)
XLA Ops:
  0.0 78.8 %shard_map.17 = f32[4,16,1024]{2,1,0:T(8,128)} custom-call(bf16[3,500,1024]{2,1,0:T(8,128)(2,1)} %half_ints.1), custom_call_target="tpu_custom_call" | custom-call | flops 9663676416 | bytes 4194304 | tf_op jit(solution)/shard_map/pallas_call | solution.py:675
  78.8 1.8 %copy.2 = f32[16,4,1024]{2,1,0:T(4,128)} copy(f32[16,4,1024]{2,0,1:T(8,128)} %bitcast.1) | data formatting | bytes 524288 | tf_op jit(solution)/shard_map/transpose | solution.py:686

commit v7 on v6

--- a/solution.py
+++ b/solution.py
@@ -381,13 +381,13 @@
 
             @pl.when(h == 1)
             def _(total=total, n=n):
-                summed[p // 2, 4 * (p % 2) + n % 2 * 2 + n // 2] = total
+                summed[p // 2, 4 * (p % 2) + n % 2 * 2 + n // 2] = total.astype(BF)
 
             @pl.when(h == 0)
             def _(total=total, n=n):
                 at = (p % 2) * 64
                 for b in range(2):
-                    summed[p // 2, n * 2 + b, :, at : at + 64] = total[:, b * 64 : b * 64 + 64]
+                    summed[p // 2, n * 2 + b, :, at : at + 64] = total[:, b * 64 : b * 64 + 64].astype(BF)
 
     ring_of = {"A": ring_a, "B": ring_b, "E": ring_e, "Q": ring_4}
     ring_of.update({f"C{i}": ring for i, ring in enumerate(rings_c)})
@@ -541,7 +541,7 @@
 
             for s in range(2):
                 for n in range(8):
-                    out_ref[s, :, n * 128 : n * 128 + 128] = pieces[n, s]
+                    out_ref[s, :, n * 128 : n * 128 + 128] = pieces[n, s].astype(F32)
 
         @pl.when(h == 0)
         def _():
@@ -550,7 +550,7 @@
                     column_piece(q, d).wait()
                 for s in range(2):
                     for n in range(4):
-                        parts = [pieces[v * 2 + s, q][:, n * 32 : n * 32 + 32] for v in range(4)]
+                        parts = [pieces[v * 2 + s, q].astype(F32)[:, n * 32 : n * 32 + 32] for v in range(4)]
                         at = q * 512 + n * 128
                         out_ref[2 + s, :, at : at + 128] = jnp.concatenate(parts, axis=1)
 
@@ -659,8 +659,8 @@
         vmem((PARTS, 4, 4, 16, 128), F32),
         vmem((PARTS, 4, 4, 16, 128), BF),
         vmem((PARTS, 3, 4, 16, 128), BF),
-        vmem((2, 8, 16, 128), F32),
-        vmem((8, 2, 16, 128), F32),
+        vmem((2, 8, 16, 128), BF),
+        vmem((8, 2, 16, 128), BF),
         vmem((1, W), F32),
         vmem((1, W), F32),
         vmem((NY - 1, 1, W), F32),

time: 80.7 us -> 80.6 us (level)
  no operation moved by 1% of the time
where the time goes in v7:
time: 80.6 us; the launch traced here: 80.4 us
  Pallas kernels  78.6 us (98%)
  local copies, waits for them, and re-layouts  1.82 us (2%)
    pallas_call x1, Pallas kernels, shards(): pl.pallas_call(kernel, out_shape=jax.ShapeDtypeStruct((4, 16, W), F32), i...  78.6 us
    transpose x1, local copies, waits for them, and re-layouts, shards(): return out.transpose(1, 0, 2)  1.82 us

profile of v7, /device:TPU:1, one launch (start us, length us, event | category | flops | bytes accessed | tf_op | source)
XLA Modules:
  0.0 80.4 jit_solution(13849253236985384990)
XLA Ops:
  0.0 78.6 %shard_map.17 = f32[4,16,1024]{2,1,0:T(8,128)} custom-call(bf16[3,500,1024]{2,1,0:T(8,128)(2,1)} %half_ints.1), custom_call_target="tpu_custom_call" | custom-call | flops 9663676416 | bytes 4194304 | tf_op jit(solution)/shard_map/pallas_call | solution.py:675
  78.6 1.8 %copy.2 = f32[16,4,1024]{2,1,0:T(4,128)} copy(f32[16,4,1024]{2,0,1:T(8,128)} %bitcast.1) | data formatting | bytes 524288 | tf_op jit(solution)/shard_map/transpose | solution.py:686
